TPU v7x, 256 devices: a whole 4x4x8 slice. The times are simulated.
256 devices in a mesh: leaf: 32 (over z, y), head: 8 (over x, core).
Axes of the slice: x: 4, y: 4, z: 8, core: 2. Of those that a mesh axis runs over, the one named last changes fastest.
Arguments:
- hidden_states: bfloat16 [8192, 4096], P('leaf', 'head'), may hold values from -6 to 6
- upper_gradient: bfloat16 [8192, 4096], P('leaf', 'head'), may hold values from -96 to 96
- w_query: bfloat16 [4096, 4096], P(None, 'head'), may hold values from -0.09375 to 0.09375
- key_projection: bfloat16 [4096, 1024], P(None, 'head'), may hold values from -0.09375 to 0.09375
- value_projection: bfloat16 [4096, 1024], P(None, 'head'), may hold values from -0.09375 to 0.09375
- query_gain: float32 [128], replicated, may hold values from 0.5 to 1.5
- key_norm_gain: float32 [128], replicated, may hold values from 0.5 to 1.5
- readout: bfloat16 [4096], P('head'), may hold values from -6 to 6
- cached_prefix_keys: bfloat16 [32, 1024, 1024], P(None, 'leaf', 'head'), may hold values from -6 to 6
- cached_prefix_values: bfloat16 [32, 1024, 1024], P(None, 'leaf', 'head'), may hold values from -6 to 6
- prefix_lengths: int32 [32], replicated, may hold values from 128 to 1024, as said below
- parents: int32 [32], P('leaf'), may hold values from 0 to 31
- visits: int32 [32], P('leaf'), may hold values from 1 to 64
Outputs:
- grad_hidden: bfloat16 [8192, 4096], P('leaf', 'head')
- grad_prefix_keys: bfloat16 [32, 1024, 1024], P(None, 'leaf', 'head')
- grad_prefix_values: bfloat16 [32, 1024, 1024], P(None, 'leaf', 'head')
Inputs may be any that keep to these rules, and one draw needn't show every extreme that they name: Node n's prefix occupies its first prefix_lengths[n] rows; some node uses all 1024 rows.
All inputs are finite; a program needn't handle non-finite values.
Results may differ from a plain program's by a relative error of at most 0.02.
Values may be sent and summed in bfloat16 or wider, within the bound.
A program may use at most 192 MiB of HBM per device.

v0:
```python
import jax
import jax.numpy as jnp
from jax import lax
from jax.sharding import PartitionSpec as P

QUERY_HEADS = 32
KEY_VALUE_HEADS = 8
HEAD_SIZE = 128


EPS = 1e-06
ROPE_BASE = 1000000.0
LOSS_SCALE = 8192.0


def rope_tables(positions, width):
    half = width // 2
    freq = ROPE_BASE ** (-2.0 * jnp.arange(half).astype(jnp.float32) / width)
    angle = positions.astype(jnp.float32)[:, None] * freq[None, :]
    return (jnp.cos(angle)[:, None, :], jnp.sin(angle)[:, None, :])


def apply_rotary(value, cosine_table, sine_table):
    half = value.shape[-1] // 2
    first, second = (value[..., :half], value[..., half:])
    return jnp.concatenate(
        [first * cosine_table - second * sine_table, second * cosine_table + first * sine_table], -1
    )


def inverse_rotary(grad, cosine_table, sine_table):
    half = grad.shape[-1] // 2
    first, second = (grad[..., :half], grad[..., half:])
    return jnp.concatenate(
        [first * cosine_table + second * sine_table, second * cosine_table - first * sine_table], -1
    )


def norm_forward(value, gain):
    inverse = lax.rsqrt(jnp.mean(value * value, axis=-1, keepdims=True) + EPS)
    return (value * inverse * gain, inverse)


def norm_reverse_pass(value, inverse, gain, grad):
    scaled = grad * gain
    return inverse * scaled - value * inverse**3 * jnp.mean(value * scaled, axis=-1, keepdims=True)


def key_mask(length, prefix_len, step_len):
    keys_at = jnp.arange(prefix_len + step_len, dtype=jnp.int32)[None, :]
    rows_at = jnp.arange(step_len, dtype=jnp.int32)[:, None]
    inside = jnp.where(keys_at < prefix_len, keys_at < length, keys_at - prefix_len <= rows_at)
    return inside.astype(jnp.float32)


def lookup(table, indices):
    match = indices[:, None] == jnp.arange(table.shape[0], dtype=jnp.int32)[None, :]
    return jnp.sum(jnp.where(match, table[None, :], jnp.zeros_like(table)[None, :]), axis=1)


def dot_rows(grads, weight):
    return lax.dot_general(
        grads, weight, (((1,), (1,)), ((), ())), preferred_element_type=jnp.float32
    )


def per_device(
    hidden_states,
    upper_gradient,
    w_query,
    key_projection,
    value_projection,
    query_gain,
    key_norm_gain,
    readout,
    cached_prefix_keys,
    cached_prefix_values,
    prefix_lengths,
    parents,
    visits,
):
    heads_per_group = QUERY_HEADS // KEY_VALUE_HEADS
    kv_local = key_projection.shape[1] // HEAD_SIZE
    q_local = kv_local * heads_per_group
    steps_local = parents.shape[0]
    row_count = hidden_states.shape[0]
    step_len = row_count // steps_local
    leaves = lax.axis_size("leaf")
    nodes = cached_prefix_keys.shape[0]
    pref_local = cached_prefix_keys.shape[1]
    width = cached_prefix_keys.shape[2]
    prefix_len = pref_local * leaves
    scale = HEAD_SIZE ** (-0.5)
    all_parents, all_visits = (
        lax.all_gather(parents, "leaf", axis=0, tiled=True),
        lax.all_gather(visits, "leaf", axis=0, tiled=True),
    )
    lengths_local = lookup(prefix_lengths, parents)
    weights = (w_query, key_projection, value_projection)
    piece = lax.all_gather(hidden_states, "head", axis=1, tiled=True)
    raw_query, unnormed_key, raw_value = tuple(
        (jnp.dot(piece, weight, preferred_element_type=jnp.float32) for weight in weights)
    )
    sibling_values = raw_value.astype(jnp.bfloat16)
    wanted_keys = jnp.take(cached_prefix_keys, all_parents, axis=0).reshape(
        leaves, steps_local, pref_local, width
    )
    wanted_values = jnp.take(cached_prefix_values, all_parents, axis=0).reshape(
        leaves, steps_local, pref_local, width
    )
    fetched_keys, fetched_values = (
        lax.all_to_all(wanted_keys, "leaf", split_axis=0, concat_axis=2, tiled=True),
        lax.all_to_all(wanted_values, "leaf", split_axis=0, concat_axis=2, tiled=True),
    )
    fetched_keys = fetched_keys.reshape(steps_local, prefix_len, kv_local, HEAD_SIZE)
    fetched_values = fetched_values.reshape(steps_local, prefix_len, kv_local, HEAD_SIZE)
    gather_heads = readout.astype(jnp.float32).reshape(kv_local, heads_per_group, HEAD_SIZE)
    step = 0
    length = lengths_local[step]
    cosine_table, sine_table = rope_tables(
        length + jnp.arange(step_len, dtype=jnp.int32), HEAD_SIZE
    )
    query_raw = raw_query.reshape(step_len, q_local, HEAD_SIZE)
    key_raw = unnormed_key.reshape(step_len, kv_local, HEAD_SIZE)
    normalized_query, inverse_q = norm_forward(query_raw, query_gain)
    normed_k, inverse_key_norm = norm_forward(key_raw, key_norm_gain)
    query_rows = (
        apply_rotary(normalized_query, cosine_table, sine_table)
        .astype(jnp.bfloat16)
        .reshape(step_len, kv_local, heads_per_group, HEAD_SIZE)
    )
    joined_keys = jnp.concatenate(
        [fetched_keys[step], apply_rotary(normed_k, cosine_table, sine_table).astype(jnp.bfloat16)],
        0,
    )
    joined_values = jnp.concatenate(
        [fetched_values[step], sibling_values.reshape(step_len, kv_local, HEAD_SIZE)], 0
    )
    mask = key_mask(length, prefix_len, step_len)
    logits = (
        jnp.einsum("tkgd,jkd->kgtj", query_rows, joined_keys, preferred_element_type=jnp.float32)
        * scale
    )
    weighted = jnp.exp(logits) * mask
    probs = weighted / jnp.sum(weighted, axis=-1, keepdims=True)
    probs_low = probs.astype(jnp.bfloat16)
    attended = jnp.einsum(
        "kgtj,jkd->kgtd", probs_low, joined_values, preferred_element_type=jnp.float32
    )
    partials = [jnp.sum(attended * gather_heads[:, :, None, :]) / step_len]
    saved = [
        (
            cosine_table,
            sine_table,
            query_raw,
            inverse_q,
            key_raw,
            inverse_key_norm,
            query_rows,
            joined_keys,
            joined_values,
            probs,
            probs_low,
            attended,
        )
    ]
    partial_scores = jnp.stack(partials)
    node_ids = jnp.arange(nodes, dtype=jnp.int32)
    owner_onehot = (all_parents[None, :] == node_ids[:, None]).astype(jnp.float32)
    local_onehot = (parents[None, :] == node_ids[:, None]).astype(jnp.float32)
    visit_totals = jnp.sum(owner_onehot * all_visits.astype(jnp.float32)[None, :], axis=1)
    step_scores = lax.psum(partial_scores, "head")
    node_totals = lax.psum(jnp.sum(local_onehot * jnp.exp(step_scores)[None, :], axis=1), "leaf")
    sibling_probs = jnp.exp(step_scores) / lookup(node_totals, parents)
    grad_scores = sibling_probs - visits.astype(jnp.float32) / lookup(visit_totals, parents)
    step = 0
    (
        cosine_table,
        sine_table,
        query_raw,
        inverse_q,
        key_raw,
        inverse_key_norm,
        query_rows,
        joined_keys,
        joined_values,
        probs,
        probs_low,
        attended,
    ) = saved[step]
    upper_layers = (
        upper_gradient.reshape(step_len, kv_local, heads_per_group, HEAD_SIZE)
        .transpose(1, 2, 0, 3)
        .astype(jnp.float32)
    )
    grad_out = (
        upper_layers + LOSS_SCALE * grad_scores[step] / step_len * gather_heads[:, :, None, :]
    )
    grad_low = grad_out.astype(jnp.bfloat16)
    grad_probs = jnp.einsum(
        "kgtd,jkd->kgtj", grad_low, joined_values, preferred_element_type=jnp.float32
    )
    delta = jnp.sum(grad_out * attended, axis=-1, keepdims=True)
    grad_logits = (probs * (grad_probs - delta) * scale).astype(jnp.bfloat16)
    grad_query = jnp.einsum(
        "kgtj,jkd->tkgd", grad_logits, joined_keys, preferred_element_type=jnp.float32
    ).reshape(step_len, q_local, HEAD_SIZE)
    full_key_gradient = jnp.einsum(
        "kgtj,tkgd->jkd", grad_logits, query_rows, preferred_element_type=jnp.float32
    )
    full_value_gradient = jnp.einsum(
        "kgtj,kgtd->jkd", probs_low, grad_low, preferred_element_type=jnp.float32
    )
    back_keys = [full_key_gradient[:prefix_len].reshape(prefix_len, width)]
    back_values = [full_value_gradient[:prefix_len].reshape(prefix_len, width)]
    query_grads = (
        norm_reverse_pass(
            query_raw, inverse_q, query_gain, inverse_rotary(grad_query, cosine_table, sine_table)
        )
        .astype(jnp.bfloat16)
        .reshape(step_len, q_local * HEAD_SIZE)
    )
    key_grads = (
        norm_reverse_pass(
            key_raw,
            inverse_key_norm,
            key_norm_gain,
            inverse_rotary(full_key_gradient[prefix_len:], cosine_table, sine_table),
        )
        .astype(jnp.bfloat16)
        .reshape(step_len, kv_local * HEAD_SIZE)
    )
    value_grads = (
        full_value_gradient[prefix_len:]
        .astype(jnp.bfloat16)
        .reshape(step_len, kv_local * HEAD_SIZE)
    )
    send_keys = jnp.stack(back_keys).reshape(steps_local, leaves, pref_local, width)
    send_values = jnp.stack(back_values).reshape(steps_local, leaves, pref_local, width)
    got_keys, got_values = (
        lax.all_to_all(send_keys, "leaf", split_axis=1, concat_axis=0, tiled=True),
        lax.all_to_all(send_values, "leaf", split_axis=1, concat_axis=0, tiled=True),
    )

    def collect_nodes(received):
        flat = received.reshape(leaves * steps_local, pref_local * width)
        summed = jnp.dot(
            owner_onehot, flat, precision=lax.Precision.HIGHEST, preferred_element_type=jnp.float32
        )
        return summed.reshape(nodes, pref_local, width).astype(jnp.bfloat16)

    grad_keys_table = collect_nodes(got_keys)
    grad_values_table = collect_nodes(got_values)
    partial_hidden = (
        dot_rows(query_grads, w_query)
        + dot_rows(key_grads, key_projection)
        + dot_rows(value_grads, value_projection)
    )
    grad_hidden = lax.psum_scatter(
        partial_hidden.astype(jnp.bfloat16), "head", scatter_dimension=1, tiled=True
    )
    return (grad_hidden, grad_keys_table, grad_values_table)


def solution(mesh):
    in_specs = (
        P("leaf", "head"),
        P("leaf", "head"),
        P(None, "head"),
        P(None, "head"),
        P(None, "head"),
        P(),
        P(),
        P("head"),
        P(None, "leaf", "head"),
        P(None, "leaf", "head"),
        P(),
        P("leaf"),
        P("leaf"),
    )
    out_specs = (P("leaf", "head"), P(None, "leaf", "head"), P(None, "leaf", "head"))
    return jax.shard_map(
        per_device, mesh=mesh, in_specs=in_specs, out_specs=out_specs, check_vma=False
    )
```

profile of v0, /device:TPU:32, one launch (start us, length us, event | category | flops | bytes accessed | tf_op | source)
XLA Modules:
  0.0 252.2 jit_solution(9655204223382231702)
XLA Ops:
  7.2 0.7 all-gather.2.cloned.1.call-update
  9.2 1.3 dynamic-slice
  10.5 0.8 dynamic-update-slice
  11.2 0.8 dynamic-update-slice.1
  12.0 22.6 %all-reduce.2 = (s32[32]{0:T(128)S(1)}, s32[32]{0:T(128)S(1)}) all-reduce(s32[32]{0:T(128)S(1)} %dynamic-update-slice, s32[32]{0:T(128)S(1)} %dynamic-update-slice.1), channel_id=1, replica_groups=mesh['leaf'=32,'head'=8] {'leaf'}, use_global_device_ids=true, to_apply=%add | all-reduce | flops 64 | bytes 512
  34.6 1.6 gather_fusion.1
  36.2 1.6 gather_fusion
  37.7 0.9 select_bitcast_fusion
  38.7 4.9 %all-to-all-start.1 = ((bf16[32,1,32,128]{3,2,1,0:T(8,128)(2,1)}), bf16[32,1,32,128]{3,2,1,0:T(8,128)(2,1)S(1)}, u32[]{:S(2)}, u32[]{:S(2)}) async-start(bf16[32,1,32,128]{3,2,1,0:T(8,128)(2,1)} %get-tuple-element.37), calls=%async_computation.1 | async-start | bytes 524288 | tf_op jit(solution)/shard_map/all_to_all | solution.py:113
  43.6 1.3 select_reduce_fusion.3
  44.9 0.6 add_convert_fusion.1
  45.6 0.7 select_reduce_fusion.1
  46.3 1.2 broadcast_bitcast_fusion
  47.5 1.3 bitcast_convert_fusion.1
  48.8 1.3 multiply_cosine_fusion
  50.1 0.7 iota_compare_fusion.2
  50.7 1.1 copy.124
  52.5 0.6 fusion.13
  53.1 1.2 all-to-all-done.1
  54.3 8.6 %all-to-all-start = ((bf16[32,1,32,128]{3,2,1,0:T(8,128)(2,1)}), bf16[32,1,32,128]{3,2,1,0:T(8,128)(2,1)}, u32[]{:S(2)}, u32[]{:S(2)}) async-start(bf16[32,1,32,128]{3,2,1,0:T(8,128)(2,1)} %get-tuple-element.38), calls=%async_computation | async-start | bytes 524288 | tf_op jit(solution)/shard_map/all_to_all | solution.py:112
  63.0 0.9 copy.125
  63.9 2.5 %fusion.14 = bf16[256,1,128]{2,0,1:T(8,128)(2,1)S(1)} fusion(bf16[256,4096]{1,0:T(8,128)(2,1)} %all-gather.2.cloned.1.call-done, bf16[4096,128]{1,0:T(8,128)(2,1)} %param.19), kind=kOutput, calls=%fused_computation.25 | convolution fusion | flops 268468224 | bytes 3211264 | tf_op jit(solution)/shard_map/dot_general | solution.py:102
  66.5 0.7 copy.126
  67.2 2.4 multiply_reduce_fusion.3
  69.7 0.6 multiply_multiply_fusion.1
  70.7 0.7 copy.122
  71.4 4.1 %fusion.66 = f32[256,512]{1,0:T(8,128)S(1)} fusion(bf16[256,4096]{1,0:T(8,128)(2,1)} %all-gather.2.cloned.1.call-done, bf16[4096,512]{1,0:T(8,128)(2,1)} %param.17), kind=kOutput, calls=%fused_computation.127 | convolution fusion | flops 1073741824 | bytes 6815744 | tf_op jit(solution)/shard_map/dot_general | solution.py:102
  75.5 1.0 reshape.426
  76.5 2.0 multiply_reduce_fusion.1
  78.5 1.0 copy.120
  79.5 0.8 copy.163
  80.3 0.9 fusion.21
  81.2 2.0 subtract_convert_fusion
  83.2 2.4 fusion.65
  85.6 0.5 fusion.11
  86.1 1.8 copy-done.1
  88.0 1.2 multiply_reduce_fusion
  89.8 13.5 %psum.14 = f32[1]{0:T(128)} all-reduce(f32[1]{0:T(128)} %bitcast.18), channel_id=1, replica_groups=mesh['leaf'=32,'head'=8] {'head'}, use_global_device_ids=true, to_apply=%region_5.7 | all-reduce | flops 1 | bytes 8 | tf_op jit(solution)/shard_map/psum | solution.py:172
  104.0 68.6 %psum.15 = f32[32]{0:T(128)S(1)} all-reduce(f32[32]{0:T(128)S(1)} %fusion.58), channel_id=1, replica_groups=mesh['leaf'=32,'head'=8] {'leaf'}, use_global_device_ids=true, to_apply=%region_6.8 | all-reduce | flops 32 | bytes 256 | tf_op jit(solution)/shard_map/psum | solution.py:173
  172.7 0.6 select_reduce_fusion.2
  173.9 2.7 %fusion.8 = f32[1280,1,128]{0,2,1:T(8,128)S(1)} fusion(bf16[1,4,256,1280]{2,3,1,0:T(8,128)(2,1)} %copy-done.1, f32[256,1,4,128]{0,3,2,1:T(8,128)S(1)} %bitcast.198, f32[4,128]{1,0:T(4,128)S(1)} %broadcast_multiply_fusion.1), kind=kOutput, calls=%fused_computation.15 | convolution fusion | flops 335806464 | bytes 3803136 | tf_op jit(solution)/shard_map/kgtj,kgtd->jkd/dot_general | solution.py:211
  176.8 3.8 %fusion.3 = bf16[4,256,1280]{1,2,0:T(8,128)(2,1)S(1)} fusion(f32[4,256]{1,0:T(4,128)S(1)} %fusion.23, f32[1,4,256,1280]{2,3,1,0:T(8,128)} %copy-done.2, f32[4,256]{1,0:T(4,128)S(1)} %get-tuple-element.41, bf16[256,1,128]{0,2,1:T(8,128)(2,1)S(1)} %copy-done.14, bf16[1024,1,128]{0,2,1:T(8,128)(2,1)} %copy.125, f32[256,1,4,128]{0,3,2,1:T(8,128)S(1)} %bitcast.200, ...), kind=kOutput, calls=%fused_computation.9 | convolution fusion | flops 343015424 | bytes 8726528 | tf_op jit(solution)/shard_map/kgtd,jkd->kgtj/dot_general | solution.py:200
  180.6 1.1 convolution_bitcast_fusion
  181.8 2.1 convolution_bitcast_fusion.1
  183.9 0.8 copy.135
  184.7 0.9 fusion.43
  185.7 0.5 copy-done.9
  186.3 1.2 multiply_add_fusion
  187.4 1.0 fusion.27
  188.5 0.8 copy.137
  189.3 1.8 fusion.46
  191.2 0.3 mul.304.clone
  192.2 1.3 convolution_add_fusion
  193.6 2.1 fusion.2
  195.7 1.0 copy.141
  196.7 11.2 %all-to-all-start.2 = ((f32[1,32,32,128]{3,2,0,1:T(8,128)}), f32[1,32,32,128]{3,2,0,1:T(8,128)S(1)}, u32[]{:S(2)}, u32[]{:S(2)}) async-start(f32[1,32,32,128]{3,2,0,1:T(8,128)} %bitcast.47), calls=%async_computation.3 | async-start | bytes 1048576 | tf_op jit(solution)/shard_map/all_to_all | solution.py:241
  208.0 1.0 copy.144
  209.0 15.3 %all-to-all-done.2 = f32[1,32,32,128]{3,2,0,1:T(8,128)S(1)} async-done(((f32[1,32,32,128]{3,2,0,1:T(8,128)}), f32[1,32,32,128]{3,2,0,1:T(8,128)S(1)}, u32[]{:S(2)}, u32[]{:S(2)}) %all-to-all-start.2) | async-done | bytes 524320 | tf_op jit(solution)/shard_map/all_to_all | solution.py:241
  224.3 6.5 %all-to-all-start.3 = ((f32[1,32,32,128]{3,2,0,1:T(8,128)}), f32[1,32,32,128]{3,2,0,1:T(8,128)S(1)}, u32[]{:S(2)}, u32[]{:S(2)}) async-start(f32[1,32,32,128]{3,2,0,1:T(8,128)} %bitcast.51), calls=%async_computation.4 | async-start | bytes 1048576 | tf_op jit(solution)/shard_map/all_to_all | solution.py:242
  230.8 0.7 convolution_convert_fusion.1
  231.5 0.8 copy.147
  232.3 11.5 %all-to-all-done.3 = f32[1,32,32,128]{3,2,0,1:T(8,128)S(1)} async-done(((f32[1,32,32,128]{3,2,0,1:T(8,128)}), f32[1,32,32,128]{3,2,0,1:T(8,128)S(1)}, u32[]{:S(2)}, u32[]{:S(2)}) %all-to-all-start.3) | async-done | bytes 524320 | tf_op jit(solution)/shard_map/all_to_all | solution.py:242
  243.9 0.7 convolution_convert_fusion
  244.6 0.8 copy.148
  (77 shorter events, 1.8 us)
Async XLA Ops:
  7.2 60.0 %copy-start = (bf16[4096,128]{1,0:T(8,128)(2,1)S(1)}, bf16[4096,128]{1,0:T(8,128)(2,1)}, u32[]{:S(2)}) copy-start(bf16[4096,128]{1,0:T(8,128)(2,1)} %param.18) | copy-start | bytes 3145732
  7.2 56.7 %all-gather.2.cloned.1.call-start = ((), (), s32[]{:S(2)}) async-start(), calls=%async_computation.5 | async-start | bytes 2359296 | tf_op jit(solution)/shard_map/all_gather | solution.py:100
  34.6 11.0 %copy-start.23 = (s32[32]{0:T(128)}, s32[32]{0:T(128)S(1)}, u32[]{:S(2)}) copy-start(s32[32]{0:T(128)S(1)} %get-tuple-element.19) | copy-start | bytes 388
  38.7 15.7 %all-to-all-start.1 = ((bf16[32,1,32,128]{3,2,1,0:T(8,128)(2,1)}), bf16[32,1,32,128]{3,2,1,0:T(8,128)(2,1)S(1)}, u32[]{:S(2)}, u32[]{:S(2)}) async-start(bf16[32,1,32,128]{3,2,1,0:T(8,128)(2,1)} %get-tuple-element.37), calls=%async_computation.1 | async-start | bytes 524288 | tf_op jit(solution)/shard_map/all_to_all | solution.py:113
  43.5 26.8 %copy-start.21 = (f32[64]{0:T(128)}, f32[64]{0:T(128)S(1)}, u32[]{:S(2)}) copy-start(f32[64]{0:T(128)S(1)} %multiply_power_fusion) | copy-start | bytes 772
  52.5 17.7 %copy-start.19 = (f32[128]{0:T(128)S(1)}, f32[128]{0:T(128)}, u32[]{:S(2)}) copy-start(f32[128]{0:T(128)} %param.21) | copy-start | bytes 1540
  54.3 28.9 %all-to-all-start = ((bf16[32,1,32,128]{3,2,1,0:T(8,128)(2,1)}), bf16[32,1,32,128]{3,2,1,0:T(8,128)(2,1)}, u32[]{:S(2)}, u32[]{:S(2)}) async-start(bf16[32,1,32,128]{3,2,1,0:T(8,128)(2,1)} %get-tuple-element.38), calls=%async_computation | async-start | bytes 524288 | tf_op jit(solution)/shard_map/all_to_all | solution.py:112
  63.0 182.4 %reduce-scatter.2.cloned.1.call-start = ((), (), s32[]{:S(2)}) async-start(), calls=%async_computation.6 | async-start | bytes 2359296 | tf_op jit(solution)/shard_map/reduce_scatter | solution.py:259
  70.2 5.3 %copy-start.15 = (f32[256]{0:T(256)}, f32[256]{0:T(256)S(1)}, u32[]{:S(2)}) copy-start(f32[256]{0:T(256)S(1)} %get-tuple-element.36) | copy-start | bytes 3076
  85.6 3.6 %copy-start.2 = (f32[1,4,256,1280]{2,3,1,0:T(8,128)}, f32[1,4,256,1280]{2,3,1,0:T(8,128)S(1)}, u32[]{:S(2)}) copy-start(f32[1,4,256,1280]{2,3,1,0:T(8,128)S(1)} %get-tuple-element.42) | copy-start | bytes 15728644
  85.6 2.4 copy-start.7
  85.6 2.4 copy-start.14
  85.6 2.4 copy-start.18
  85.6 88.2 %copy-start.22 = (bf16[512]{0:T(512)(128)(2,1)S(1)}, bf16[512]{0:T(512)(128)(2,1)}, u32[]{:S(2)}) copy-start(bf16[512]{0:T(512)(128)(2,1)} %param.22) | copy-start | bytes 3076
  86.1 1.8 copy-start.1
  176.7 3.9 %copy-start.5 = (bf16[256,4,64]{2,0,1:T(8,128)(2,1)S(1)}, bf16[256,4,64]{2,0,1:T(8,128)(2,1)}, u32[]{:S(2)}) copy-start(bf16[256,4,64]{2,0,1:T(8,128)(2,1)} %get-tuple-element.25) | copy-start | bytes 393220
  176.8 3.9 %copy-start.6 = (bf16[256,4,64]{2,0,1:T(8,128)(2,1)S(1)}, bf16[256,4,64]{2,0,1:T(8,128)(2,1)}, u32[]{:S(2)}) copy-start(bf16[256,4,64]{2,0,1:T(8,128)(2,1)} %get-tuple-element.26) | copy-start | bytes 393220
  176.8 5.0 %copy-start.8 = (bf16[256,1,128]{2,0,1:T(8,128)(2,1)S(1)}, bf16[256,1,128]{2,0,1:T(8,128)(2,1)}, u32[]{:S(2)}) copy-start(bf16[256,1,128]{2,0,1:T(8,128)(2,1)} %copy.122) | copy-start | bytes 196612
  180.6 5.0 %copy-start.20 = (f32[128]{0:T(128)S(1)}, f32[128]{0:T(128)}, u32[]{:S(2)}) copy-start(f32[128]{0:T(128)} %param.21) | copy-start | bytes 1540
  181.8 7.5 %copy-start.16 = (f32[256]{0:T(256)S(1)}, f32[256]{0:T(256)}, u32[]{:S(2)}) copy-start(f32[256]{0:T(256)} %copy-done.15) | copy-start | bytes 3076
  185.6 0.6 copy-start.9
  185.6 0.6 copy-start.10
  188.5 3.7 %copy-start.17 = (f32[512]{0:T(512)S(1)}, f32[512]{0:T(512)}, u32[]{:S(2)}) copy-start(f32[512]{0:T(512)} %broadcast_bitcast_fusion) | copy-start | bytes 6148
  189.3 1.9 copy-start.11
  189.3 2.2 copy-start.12
  189.3 2.5 %copy-start.13 = (f32[256,4]{1,0:T(8,128)S(1)}, f32[256,4]{1,0:T(8,128)}, u32[]{:S(2)}) copy-start(f32[256,4]{1,0:T(8,128)} %copy.137) | copy-start | bytes 12292
  189.3 2.9 %copy-start.4 = (bf16[4096,512]{1,0:T(8,128)(2,1)S(1)}, bf16[4096,512]{1,0:T(8,128)(2,1)}, u32[]{:S(2)}) copy-start(bf16[4096,512]{1,0:T(8,128)(2,1)} %param.17) | copy-start | bytes 12582916
  192.2 1.4 copy-start.3
  195.7 35.1 %copy-start.24 = (s32[32]{0:T(128)S(1)}, s32[32]{0:T(128)}, u32[]{:S(2)}) copy-start(s32[32]{0:T(128)} %copy-done.23) | copy-start | bytes 388
  196.7 27.6 %all-to-all-start.2 = ((f32[1,32,32,128]{3,2,0,1:T(8,128)}), f32[1,32,32,128]{3,2,0,1:T(8,128)S(1)}, u32[]{:S(2)}, u32[]{:S(2)}) async-start(f32[1,32,32,128]{3,2,0,1:T(8,128)} %bitcast.47), calls=%async_computation.3 | async-start | bytes 1048576 | tf_op jit(solution)/shard_map/all_to_all | solution.py:241
  224.3 19.5 %all-to-all-start.3 = ((f32[1,32,32,128]{3,2,0,1:T(8,128)}), f32[1,32,32,128]{3,2,0,1:T(8,128)S(1)}, u32[]{:S(2)}, u32[]{:S(2)}) async-start(f32[1,32,32,128]{3,2,0,1:T(8,128)} %bitcast.51), calls=%async_computation.4 | async-start | bytes 1048576 | tf_op jit(solution)/shard_map/all_to_all | solution.py:242
Sparse Core Ops, SparseCore 0:
  9.9 30.2 all-gather.1
  195.8 36.6 reduce-scatter.1
where the time goes:
time: 253 us; the launch traced here: 252 us
  blocking collectives  105 us (42%)
  starting transfers between devices  31.2 us (12%)
  matrix products  29 us (11%)
  waiting for transfers between devices  28.8 us (11%)
  local copies, waits for them, and re-layouts  22.1 us (9%)
  between operations  18.5 us (7%)
  other arithmetic  17.8 us (7%)
    psum x1, blocking collectives, per_device(): lax.psum(jnp.sum(local_onehot * jnp.exp(step_scores)[None, :], axis=1), '...  68.6 us
    unnamed x1, blocking collectives  22.6 us
    all_to_all x1, waiting for transfers between devices, per_device(): lax.all_to_all(send_keys, 'leaf', split_axis=1, concat_axis=0, tiled=True)  15.3 us
    psum x1, blocking collectives, per_device(): step_scores = lax.psum(partial_scores, 'head')  13.5 us
    all_to_all x1, waiting for transfers between devices, per_device(): lax.all_to_all(send_values, 'leaf', split_axis=1, concat_axis=0, tiled=True)  11.5 us
    all_to_all x1, starting transfers between devices, per_device(): lax.all_to_all(send_keys, 'leaf', split_axis=1, concat_axis=0, tiled=True)  11.2 us
    dot_general x3, matrix products, per_device(): jnp.dot(piece, weight, preferred_element_type=jnp.float32)  9.04 us
    all_to_all x1, starting transfers between devices, per_device(): lax.all_to_all(wanted_keys, 'leaf', split_axis=0, concat_axis=2, tiled=True)  8.62 us
  transfers between devices with their start and end apart: 6, of which 3 were waited for; matrix products, arithmetic and copies ran while one was open for 16% of the time, Pallas kernels for 0%

commit v1 on v0

v1 whole, which is shorter than its diff:
```python
import functools

import jax
import jax.numpy as jnp
import numpy as np
from jax import lax
from jax.experimental import pallas as pl
from jax.experimental.pallas import tpu as pltpu
from jax.sharding import PartitionSpec as P

HEAD_SIZE = 128
GROUP = 4
EPS = 1e-06
ROPE_BASE = 1000000.0
LOSS_SCALE = 8192.0
SCALE = HEAD_SIZE ** (-0.5)
BF16 = jnp.bfloat16
F32 = jnp.float32


def dot_nn(a, b):
    return lax.dot_general(a, b, (((1,), (0,)), ((), ())), preferred_element_type=F32)


def dot_nt(a, b):
    return lax.dot_general(a, b, (((1,), (1,)), ((), ())), preferred_element_type=F32)


def dot_tn(a, b):
    return lax.dot_general(a, b, (((0,), (0,)), ((), ())), preferred_element_type=F32)


def z_offsets(nz):
    order = [0]
    for step in range(1, nz // 2 + 1):
        order.append(step)
        if len(order) < nz:
            order.append(-step)
    return order


def main_kernel(
    ny,
    parents,
    visits,
    lengths,
    freq,
    hid,
    upper,
    wq,
    wk,
    wv,
    qgain,
    kgain,
    readout,
    ck,
    cv,
    gh_out,
    got_out,
    par_out,
    w,
    hf,
    cks,
    cvs,
    up,
    urb,
    par,
    par_s,
    kvs,
    kvf,
    acc,
    cosb,
    sinb,
    q,
    own,
    e,
    uv,
    rv,
    lsum,
    asum,
    bsum,
    dv,
    dqt,
    sch,
    scl,
    gs,
    gr,
    g768,
    sib_s,
    sib_r,
    ps,
    rs_s,
    rs_r,
    in_sem,
    par_send,
    par_recv,
    s_sem,
    kv_send,
    kv_recv,
    ag_send,
    ag_recv,
    sch_send,
    sch_recv,
    scl_send,
    scl_recv,
    g_send,
    g_recv,
    sb_send,
    sb_recv,
    rs_send,
    rs_recv,
):
    me_l = lax.axis_index("leaf")
    me_g = lax.axis_index("head")
    nl = lax.axis_size("leaf")
    ng = lax.axis_size("head")
    nz = nl // ny
    nx = ng // 2
    z, y = me_l // ny, me_l % ny
    x, core = me_g // 2, me_g % 2
    nodes, rows, width = ck.shape
    tokens, feats = hid.shape
    half = tokens // 2

    def chip(dx, other=False):
        side = 1 - core if other else core
        return ((x + dx + nx) % nx) * 2 + side

    def leaf_at(dz, dy):
        return ((z + dz + nz) % nz) * ny + (y + dy + ny) % ny

    def remote(src, dst, send, recv, **target):
        return pltpu.make_async_remote_copy(
            src_ref=src,
            dst_ref=dst,
            send_sem=send,
            recv_sem=recv,
            device_id=target,
            device_id_type=pl.DeviceIdType.MESH,
        )

    loads = [
        pltpu.make_async_copy(hid, hf.at[me_g], in_sem.at[0]),
        pltpu.make_async_copy(ck, cks, in_sem.at[1]),
        pltpu.make_async_copy(cv, cvs, in_sem.at[2]),
        pltpu.make_async_copy(wq, w.at[:, pl.ds(0, GROUP * width)], in_sem.at[3]),
        pltpu.make_async_copy(wk, w.at[:, pl.ds(GROUP * width, width)], in_sem.at[4]),
        pltpu.make_async_copy(wv, w.at[:, pl.ds((GROUP + 1) * width, width)], in_sem.at[5]),
        pltpu.make_async_copy(upper, up, in_sem.at[6]),
    ]
    for load in loads:
        load.start()

    barrier = pltpu.get_barrier_semaphore()

    def greet_leaf(o, c):
        pl.semaphore_signal(
            barrier, inc=1, device_id={"leaf": (me_l + o) % nl}, device_id_type=pl.DeviceIdType.MESH
        )
        return c

    def greet_head(o, c):
        pl.semaphore_signal(
            barrier, inc=1, device_id={"head": (me_g + o) % ng}, device_id_type=pl.DeviceIdType.MESH
        )
        return c

    lax.fori_loop(1, nl, greet_leaf, 0)
    lax.fori_loop(1, ng, greet_head, 0)
    lane = lax.broadcasted_iota(jnp.int32, (1, 1, 128), 2)
    par[pl.ds(me_l, 1)] = jnp.where(lane < 64, parents[0], visits[0])
    pl.semaphore_wait(barrier, nl - 1 + ng - 1)

    def par_copy(o):
        return remote(
            par.at[me_l],
            par.at[me_l],
            par_send.at[o],
            par_recv.at[me_l],
            leaf=(me_l + o) % nl,
        )

    def par_start(o, c):
        par_copy(o).start()
        return c

    lax.fori_loop(1, nl, par_start, 0)

    loads[0].wait()

    def ag_copy(sem, block, part, target):
        rows_at = hf.at[block, pl.ds(part * half, half)]
        return remote(rows_at, rows_at, ag_send.at[sem], ag_recv.at[block, part], head=target)

    def ag_wait(block, part):
        rows_at = hf.at[block, pl.ds(part * half, half)]
        remote(rows_at, rows_at, ag_send.at[0], ag_recv.at[block, part], head=me_g).wait_recv()

    right, left, sibling = chip(1), chip(-1), chip(0, True)
    ag = [
        ag_copy(0, me_g, 0, right),
        ag_copy(1, me_g, 1, left),
        ag_copy(2, me_g, 1, right),
        ag_copy(3, me_g, 0, left),
        ag_copy(4, me_g, 0, sibling),
        ag_copy(5, me_g, 1, sibling),
    ]
    for copy in ag:
        copy.start()

    def par_arrive(o, c):
        src = (me_l + o) % nl
        remote(par.at[src], par.at[src], par_send.at[o], par_recv.at[src], leaf=src).wait_recv()
        return c

    lax.fori_loop(1, nl, par_arrive, 0)
    to_smem = pltpu.make_async_copy(par, par_s, s_sem)
    to_smem.start()
    loads[1].wait()
    loads[2].wait()
    to_smem.wait()
    order = z_offsets(nz)
    pairs = [(order[2 * i], order[2 * i + 1]) for i in range(nz // 2)]

    def kv_copy(i, dest):
        return remote(kvs.at[i], kvf.at[me_l], kv_send.at[i], kv_recv.at[me_l], leaf=dest)

    kv_copies = []
    slot = 0
    for dz in order:
        for dy in range(ny):
            dest = leaf_at(-dz, -dy)
            node = par_s[dest, 0, 0]
            if dz == 0 and dy == 0:
                kvf[me_l, 0] = cks[node]
                kvf[me_l, 1] = cvs[node]
            else:
                kvs[slot, 0] = cks[node]
                kvs[slot, 1] = cvs[node]
                copy = kv_copy(slot, dest)
                copy.start()
                kv_copies.append(copy)
                slot += 1

    length = lengths[parents[0]]
    position = (length + lax.broadcasted_iota(jnp.int32, (tokens, width), 0)).astype(F32)
    angle = position * freq[...]
    cosb[...] = jnp.cos(angle)
    low = lax.broadcasted_iota(jnp.int32, (tokens, width), 1) < width // 2
    sine = jnp.sin(angle)
    sinb[...] = jnp.where(low, -sine, sine)

    def rotate(value):
        return value * cosb[...] + pltpu.roll(value, width // 2, 1) * sinb[...]

    def rotate_back(value):
        return value * cosb[...] - pltpu.roll(value, width // 2, 1) * sinb[...]

    loads[6].wait()
    read = readout[...]
    for h in range(GROUP):
        cols = slice(h * width, (h + 1) * width)
        urb[h, :, 0:width] = up[:, cols]
        urb[h, :, width : 2 * width] = jnp.broadcast_to(
            read[:, cols].astype(F32), (tokens, width)
        ).astype(BF16)
    read_rows = jnp.concatenate(
        [read[:, h * width : (h + 1) * width].astype(F32) for h in range(GROUP)]
        + [jnp.zeros((16 - GROUP, width), F32)],
        0,
    ).astype(BF16)

    for i in (3, 4, 5):
        loads[i].wait()

    def project(block, first=False):
        part = dot_nn(hf[block], w[pl.ds(pl.multiple_of(block * feats, feats), feats), :])
        if first:
            acc[...] = part
        else:
            acc[...] += part

    project(me_g, True)
    ag_wait(left, 0)
    more = [ag_copy(6, left, 0, right), ag_copy(7, left, 0, sibling)]
    for copy in more:
        copy.start()
    ag_wait(right, 1)
    more2 = [ag_copy(8, right, 1, left), ag_copy(9, right, 1, sibling)]
    for copy in more2:
        copy.start()
    ag_wait(sibling, 0)
    ag_wait(sibling, 1)
    project(sibling)
    ag_wait(left, 1)
    ag_wait(right, 0)
    more3 = [ag_copy(10, left, 1, sibling), ag_copy(11, right, 0, sibling)]
    for copy in more3:
        copy.start()
    project(left)
    project(right)
    opposite = chip(2)
    ag_wait(opposite, 0)
    more4 = [ag_copy(12, opposite, 0, sibling)]
    more4[0].start()
    ag_wait(opposite, 1)
    more4.append(ag_copy(13, opposite, 1, sibling))
    more4[1].start()
    project(opposite)
    for dx in (-1, 1, 2):
        block = chip(dx, True)
        ag_wait(block, 0)
        ag_wait(block, 1)
        project(block)
    ag += more + more2 + more3 + more4

    def norm_inverse(raw):
        return lax.rsqrt(jnp.mean(raw * raw, axis=-1, keepdims=True) + EPS)

    for h in range(GROUP + 1):
        raw = acc[:, h * width : (h + 1) * width]
        gain = qgain[...] if h < GROUP else kgain[...]
        turned = rotate(raw * norm_inverse(raw) * gain).astype(BF16)
        if h < GROUP:
            q[h] = turned
        else:
            own[0] = turned
    own[1] = acc[:, (GROUP + 1) * width :].astype(BF16)

    def keys_of(i):
        if i == 0:
            return own[0]
        za, zb = [((z + dz + nz) % nz) * ny for dz in pairs[i - 1]]
        return jnp.concatenate(
            [kvf[pl.ds(zz, ny), 0].reshape(ny * rows, width) for zz in (za, zb)], 0
        )

    def values_of(i):
        if i == 0:
            return own[1]
        za, zb = [((z + dz + nz) % nz) * ny for dz in pairs[i - 1]]
        return jnp.concatenate(
            [kvf[pl.ds(zz, ny), 1].reshape(ny * rows, width) for zz in (za, zb)], 0
        )

    chunks = len(pairs) + 1

    def forward(i):
        keys, values = keys_of(i), values_of(i)
        count = keys.shape[0]
        at = lax.broadcasted_iota(jnp.int32, (count, tokens), 0)
        if i == 0:
            mask = at <= lax.broadcasted_iota(jnp.int32, (count, tokens), 1)
        else:
            za, zb = [((z + dz + nz) % nz) * ny * rows for dz in pairs[i - 1]]
            mask = jnp.where(at < ny * rows, at + za, at - ny * rows + zb) < length
        for h in range(GROUP):
            weight = jnp.where(mask, jnp.exp(dot_nt(keys, q[h]) * SCALE), 0.0)
            total = jnp.sum(weight, axis=0, keepdims=True)
            if i == 0:
                lsum[h : h + 1, :] = total
            else:
                lsum[h : h + 1, :] += total
            e[i, h] = weight
            uv[i, h] = dot_nt(values, up[:, h * width : (h + 1) * width])
        rv[i] = dot_nt(values, read_rows)

    forward(0)
    for i in range(1, chunks):
        for dz in pairs[i - 1]:
            for dy in range(ny):
                if dz == 0 and dy == 0:
                    continue
                src = leaf_at(dz, dy)
                remote(
                    kvf.at[src], kvf.at[src], kv_send.at[0], kv_recv.at[src], leaf=src
                ).wait_recv()
        forward(i)

    score = jnp.zeros((1, 1), F32)
    for h in range(GROUP):
        inverse = 1.0 / lsum[h : h + 1, :]
        a = jnp.zeros((1, tokens), F32)
        b = jnp.zeros((1, tokens), F32)
        for i in range(chunks):
            prob = e[i, h] * inverse
            e[i, h] = prob
            a += jnp.sum(prob * rv[i][:, h : h + 1], axis=0, keepdims=True)
            b += jnp.sum(prob * uv[i, h], axis=0, keepdims=True)
        asum[h : h + 1, :] = a
        bsum[h : h + 1, :] = b
        score += jnp.sum(a, axis=1, keepdims=True)
    sch[pl.ds(me_g, 1)] = jnp.broadcast_to((score / tokens)[None], (1, 1, 128))

    def sch_copy(o):
        return remote(
            sch.at[me_g], sch.at[me_g], sch_send.at[o], sch_recv.at[me_g], head=(me_g + o) % ng
        )

    def scl_copy(o):
        return remote(
            scl.at[me_l], scl.at[me_l], scl_send.at[o], scl_recv.at[me_l], leaf=(me_l + o) % nl
        )

    for o in range(1, ng):
        sch_copy(o).start()

    def value_grads(i):
        total = None
        for h in range(GROUP):
            term = dot_nn(e[i, h].astype(BF16), urb[h])
            total = term if total is None else total + term
        dv[i] = total

    for i in range(chunks // 2):
        value_grads(i)
    for o in range(1, ng):
        src = (me_g + o) % ng
        remote(sch.at[src], sch.at[src], sch_send.at[o], sch_recv.at[src], head=src).wait_recv()
    scl[pl.ds(me_l, 1)] = jnp.sum(sch[...], axis=0, keepdims=True)

    def scl_start(o, c):
        scl_copy(o).start()
        return c

    lax.fori_loop(1, nl, scl_start, 0)
    for i in range(chunks // 2, chunks):
        value_grads(i)

    def scl_arrive(o, c):
        src = (me_l + o) % nl
        remote(scl.at[src], scl.at[src], scl_send.at[o], scl_recv.at[src], leaf=src).wait_recv()
        return c

    lax.fori_loop(1, nl, scl_arrive, 0)

    node_at = lax.broadcasted_iota(jnp.int32, (nl, 1, 128), 2)
    table = par[...]
    hot = jnp.where(table == node_at, 1.0, 0.0) * jnp.where(node_at < nodes, 1.0, 0.0)
    seen = pltpu.roll(table.reshape(nl, 128), 64, 1).reshape(nl, 1, 128).astype(F32)
    seen = jnp.sum(jnp.where(node_at == 0, seen, 0.0), axis=2, keepdims=True)
    grown = jnp.exp(scl[...])
    node_total = jnp.sum(hot * grown, axis=0, keepdims=True)
    node_seen = jnp.sum(hot * seen, axis=0, keepdims=True)
    mine = (lax.broadcasted_iota(jnp.int32, (nl, 1, 128), 0) == me_l).astype(F32)
    own_hot = jnp.sum(hot * mine, axis=0)
    own_total = jnp.sum(own_hot * node_total[0], axis=1, keepdims=True)
    own_seen = jnp.sum(own_hot * node_seen[0], axis=1, keepdims=True)
    own_grown = jnp.sum(jnp.where(lane[0] == 0, jnp.sum(grown * mine, axis=0), 0.0), axis=1, keepdims=True)
    own_visits = jnp.sum(jnp.where(lane[0] == 0, jnp.sum(seen * mine, axis=0), 0.0), axis=1, keepdims=True)
    c = (LOSS_SCALE / tokens) * (own_grown / own_total - own_visits / own_seen)

    g_copies = []
    for i in list(range(1, chunks)) + [0]:
        keys = keys_of(i)
        grad_keys = None
        for h in range(GROUP):
            shift = bsum[h : h + 1, :] + c * asum[h : h + 1, :]
            grad = uv[i, h] + c * rv[i][:, h : h + 1] - shift
            grad = (e[i, h] * grad * SCALE).astype(BF16)
            term = dot_nn(grad, q[h])
            grad_keys = term if grad_keys is None else grad_keys + term
            back = dot_tn(keys, grad)
            if i == 1:
                dqt[h] = back
            else:
                dqt[h] += back
        grad_values = dv[i][:, :width] + c * dv[i][:, width:]
        if i == 0:
            step_grad_keys, step_grad_values = grad_keys, grad_values
            continue
        for j, dz in enumerate(pairs[i - 1]):
            zz = ((z + dz + nz) % nz) * ny
            part = slice(j * ny * rows, (j + 1) * ny * rows)
            gs[pl.ds(zz, ny), 0] = grad_keys[part].astype(BF16).reshape(ny, rows, width)
            gs[pl.ds(zz, ny), 1] = grad_values[part].astype(BF16).reshape(ny, rows, width)
            for dy in range(ny):
                dest = leaf_at(dz, dy)
                if dz == 0 and dy == 0:
                    gr[me_l] = gs[me_l]
                else:
                    copy = remote(
                        gs.at[dest], gr.at[me_l], g_send.at[len(g_copies)], g_recv.at[me_l], leaf=dest
                    )
                    copy.start()
                    g_copies.append(copy)

    def norm_back(raw, gain, grad):
        inverse = norm_inverse(raw)
        scaled = grad * gain
        mean = jnp.mean(raw * scaled, axis=-1, keepdims=True)
        return (inverse * scaled - raw * (inverse * inverse * inverse) * mean).astype(BF16)

    for h in range(GROUP):
        cols = slice(h * width, (h + 1) * width)
        g768[:, cols] = norm_back(acc[:, cols], qgain[...], rotate_back(dqt[h].T))
    cols = slice(GROUP * width, (GROUP + 1) * width)
    g768[:, cols] = norm_back(acc[:, cols], kgain[...], rotate_back(step_grad_keys))
    g768[:, (GROUP + 1) * width :] = step_grad_values.astype(BF16)

    def term(block):
        return dot_nt(g768[...], w[pl.ds(pl.multiple_of(block * feats, feats), feats), :])

    sb_copies = []
    hops = (2, 1, -1, 0)
    for j, dx in enumerate(hops):
        sib_s[j] = term(chip(dx, True)).astype(BF16)
        copy = remote(sib_s.at[j], sib_r.at[j], sb_send.at[j], sb_recv.at[j], head=sibling)
        copy.start()
        sb_copies.append(copy)
        ps[j] = term(chip(dx)).astype(BF16).astype(F32)

    def join(j):
        remote(sib_s.at[j], sib_r.at[j], sb_send.at[j], sb_recv.at[j], head=sibling).wait_recv()
        ps[j] += sib_r[j].astype(F32)

    def rs_copy(slot, target):
        return remote(rs_s.at[slot], rs_r.at[slot], rs_send.at[slot], rs_recv.at[slot], head=target)

    first, second = slice(0, half), slice(half, tokens)
    join(0)
    rs_s[0] = ps[0, first].astype(BF16)
    rs_s[1] = ps[0, second].astype(BF16)
    rs_copies = [rs_copy(0, right), rs_copy(1, left)]
    rs_copies[0].start()
    rs_copies[1].start()
    join(1)
    rs_s[2] = ps[1, second].astype(BF16)
    rs_copies.append(rs_copy(2, right))
    rs_copies[2].start()
    join(2)
    rs_s[3] = ps[2, first].astype(BF16)
    rs_copies.append(rs_copy(3, left))
    rs_copies[3].start()
    rs_copies[0].wait_recv()
    rs_s[4] = (ps[1, first] + rs_r[0].astype(F32)).astype(BF16)
    rs_copies.append(rs_copy(4, right))
    rs_copies[4].start()
    rs_copies[1].wait_recv()
    rs_s[5] = (ps[2, second] + rs_r[1].astype(F32)).astype(BF16)
    rs_copies.append(rs_copy(5, left))
    rs_copies[5].start()
    join(3)
    for slot in range(2, 6):
        rs_copies[slot].wait_recv()
    gh_out[first, :] = (ps[3, first] + rs_r[4].astype(F32) + rs_r[3].astype(F32)).astype(BF16)
    gh_out[second, :] = (ps[3, second] + rs_r[2].astype(F32) + rs_r[5].astype(F32)).astype(BF16)

    for dz in order:
        for dy in range(ny):
            if dz == 0 and dy == 0:
                continue
            src = leaf_at(-dz, -dy)
            remote(gr.at[src], gr.at[src], g_send.at[0], g_recv.at[src], leaf=src).wait_recv()
    got_out[...] = gr[...]
    par_out[...] = par[...]

    for copy in ag + kv_copies + sb_copies + rs_copies + g_copies:
        copy.wait_send()
    for o in range(1, ng):
        sch_copy(o).wait_send()

    def small_sent(o, c):
        par_copy(o).wait_send()
        scl_copy(o).wait_send()
        return c

    lax.fori_loop(1, nl, small_sent, 0)


def collect_kernel(par, got, gh_in, gh, gk, gv, total):
    total[...] = jnp.zeros_like(total)

    def add(s, c):
        node = par[s, 0, 0]
        total[node] += got[s].astype(F32)
        return c

    lax.fori_loop(0, got.shape[0], add, 0)
    gk[...] = total[:, 0].astype(BF16)
    gv[...] = total[:, 1].astype(BF16)
    gh[...] = gh_in[...]


def per_device(
    ny,
    hidden_states,
    upper_gradient,
    w_query,
    key_projection,
    value_projection,
    query_gain,
    key_norm_gain,
    readout,
    cached_prefix_keys,
    cached_prefix_values,
    prefix_lengths,
    parents,
    visits,
):
    nl, ng = lax.axis_size("leaf"), lax.axis_size("head")
    nodes, rows, width = cached_prefix_keys.shape
    tokens, feats = hidden_states.shape
    model = w_query.shape[0]
    nz = nl // ny
    chunks = nz // 2 + 1
    span = max(2 * ny * rows, tokens)
    half = tokens // 2
    cols = (GROUP + 2) * width
    inverse = np.asarray(
        ROPE_BASE ** (-2.0 * (np.arange(width) % (width // 2)) / width), np.float32
    ).reshape(1, width)
    smem = pl.BlockSpec(memory_space=pltpu.SMEM)
    vmem = pl.BlockSpec(memory_space=pltpu.VMEM)
    anywhere = pl.BlockSpec(memory_space=pl.ANY)
    dma = pltpu.SemaphoreType.DMA
    scratch = [
        pltpu.VMEM((model, cols), BF16),
        pltpu.VMEM((ng, tokens, feats), BF16),
        pltpu.VMEM((nodes, rows, width), BF16),
        pltpu.VMEM((nodes, rows, width), BF16),
        pltpu.VMEM((tokens, GROUP * width), BF16),
        pltpu.VMEM((GROUP, tokens, 2 * width), BF16),
        pltpu.VMEM((nl, 1, 128), jnp.int32),
        pltpu.SMEM((nl, 1, 128), jnp.int32),
        pltpu.VMEM((nl, 2, rows, width), BF16),
        pltpu.VMEM((nl, 2, rows, width), BF16),
        pltpu.VMEM((tokens, cols), F32),
        pltpu.VMEM((tokens, width), F32),
        pltpu.VMEM((tokens, width), F32),
        pltpu.VMEM((GROUP, tokens, width), BF16),
        pltpu.VMEM((2, tokens, width), BF16),
        pltpu.VMEM((chunks, GROUP, span, tokens), F32),
        pltpu.VMEM((chunks, GROUP, span, tokens), F32),
        pltpu.VMEM((chunks, span, 16), F32),
        pltpu.VMEM((GROUP, tokens), F32),
        pltpu.VMEM((GROUP, tokens), F32),
        pltpu.VMEM((GROUP, tokens), F32),
        pltpu.VMEM((chunks, span, 2 * width), F32),
        pltpu.VMEM((GROUP, width, tokens), F32),
        pltpu.VMEM((ng, 1, 128), F32),
        pltpu.VMEM((nl, 1, 128), F32),
        pltpu.VMEM((nl, 2, rows, width), BF16),
        pltpu.VMEM((nl, 2, rows, width), BF16),
        pltpu.VMEM((tokens, cols), BF16),
        pltpu.VMEM((4, tokens, feats), BF16),
        pltpu.VMEM((4, tokens, feats), BF16),
        pltpu.VMEM((4, tokens, feats), F32),
        pltpu.VMEM((6, half, feats), BF16),
        pltpu.VMEM((6, half, feats), BF16),
        dma((7,)),
        dma((nl,)),
        dma((nl,)),
        dma,
        dma((nl,)),
        dma((nl,)),
        dma((14,)),
        dma((ng, 2)),
        dma((ng,)),
        dma((ng,)),
        dma((nl,)),
        dma((nl,)),
        dma((nl,)),
        dma((nl,)),
        dma((4,)),
        dma((4,)),
        dma((6,)),
        dma((6,)),
    ]
    gh, got, par = pl.pallas_call(
        functools.partial(main_kernel, ny),
        out_shape=(
            jax.ShapeDtypeStruct((tokens, feats), BF16),
            jax.ShapeDtypeStruct((nl, 2, rows, width), BF16),
            jax.ShapeDtypeStruct((nl, 1, 128), jnp.int32),
        ),
        in_specs=[smem, smem, smem, vmem]
        + [anywhere] * 5
        + [vmem] * 3
        + [anywhere] * 2,
        out_specs=(vmem, vmem, vmem),
        scratch_shapes=scratch,
        compiler_params=pltpu.CompilerParams(
            collective_id=0, has_side_effects=True, vmem_limit_bytes=58 * 1024 * 1024
        ),
    )(
        parents,
        visits,
        prefix_lengths,
        jnp.asarray(inverse),
        hidden_states,
        upper_gradient,
        w_query,
        key_projection,
        value_projection,
        query_gain.reshape(1, width),
        key_norm_gain.reshape(1, width),
        readout.reshape(1, GROUP * width),
        cached_prefix_keys,
        cached_prefix_values,
    )
    table = jax.ShapeDtypeStruct((nodes, rows, width), BF16)
    return pl.pallas_call(
        collect_kernel,
        out_shape=(jax.ShapeDtypeStruct((tokens, feats), BF16), table, table),
        in_specs=[smem, vmem, vmem],
        out_specs=(vmem, vmem, vmem),
        scratch_shapes=[pltpu.VMEM((nodes, 2, rows, width), F32)],
    )(par, got, gh)


def solution(mesh):
    in_specs = (
        P("leaf", "head"),
        P("leaf", "head"),
        P(None, "head"),
        P(None, "head"),
        P(None, "head"),
        P(),
        P(),
        P("head"),
        P(None, "leaf", "head"),
        P(None, "leaf", "head"),
        P(),
        P("leaf"),
        P("leaf"),
    )
    out_specs = (P("leaf", "head"), P(None, "leaf", "head"), P(None, "leaf", "head"))
    ny = 4 if mesh.shape["leaf"] == 32 else 1
    return jax.shard_map(
        functools.partial(per_device, ny),
        mesh=mesh,
        in_specs=in_specs,
        out_specs=out_specs,
        check_vma=False,
    )
```

time: 253 us -> 70.5 us (0.28)
  blocking collectives: 105 us -> 0 us
  Pallas kernels: 0 us -> 67.1 us
  starting transfers between devices: 31.2 us -> 0 us
  matrix products: 29 us -> 0 us
  waiting for transfers between devices: 28.8 us -> 0 us
  local copies, waits for them, and re-layouts: 22.1 us -> 1.26 us
  other arithmetic: 17.8 us -> 0 us
  between operations: 18.5 us -> 1.93 us
    psum x2 -> x0, blocking collectives: 82.2 us -> none  [the longest x1 68.6 us: per_device(): lax.psum(jnp.sum(local_onehot * jnp.exp(step_scores)[None, :], axis=1), '...]
    pallas_call x0 -> x2, Pallas kernels: none -> 67.1 us  [the longest x1 64.7 us: per_device(): pl.pallas_call(functools.partial(main_kernel, ny), out_shape=(jax.ShapeDt...]
    all_to_all x4 -> x0, starting transfers between devices: 31.1 us -> none  [the longest x1 11.2 us: per_device(): lax.all_to_all(send_keys, 'leaf', split_axis=1, concat_axis=0, tiled=True)]
    dot_general x14 -> x0, matrix products: 29 us -> none  [the longest x3 9.04 us: per_device(): jnp.dot(piece, weight, preferred_element_type=jnp.float32)]
    all_to_all x4 -> x0, waiting for transfers between devices: 28.1 us -> none  [the longest x1 15.3 us: per_device(): lax.all_to_all(send_keys, 'leaf', split_axis=1, concat_axis=0, tiled=True)]
    unnamed x1 -> x0, blocking collectives: 22.6 us -> none
    unnamed x58 -> x0, local copies, waits for them, and re-layouts: 7.65 us -> none
    reduce_sum x7 -> x0, other arithmetic: 4.95 us -> none  [the longest x3 2.53 us: lookup(): jnp.sum(jnp.where(match, table[None, :], jnp.zeros_like(table)[None, :]),...]
  transfers between devices with their start and end apart: 6 -> 0, of which waited for: 3 -> 0; matrix products, arithmetic and copies ran while one was open for 16% -> 0% of each run, Pallas kernels for 0% -> 0%
where the time goes in v1:
time: 70.5 us; the launch traced here: 70.3 us
  Pallas kernels  67.1 us (95%)
  between operations  1.93 us (3%)
  local copies, waits for them, and re-layouts  1.26 us (2%)
    pallas_call x1, Pallas kernels, per_device(): pl.pallas_call(functools.partial(main_kernel, ny), out_shape=(jax.ShapeDt...  64.7 us
    pallas_call x1, Pallas kernels, per_device(): pl.pallas_call(collect_kernel, out_shape=(jax.ShapeDtypeStruct((tokens, f...  2.36 us

profile of v1, /device:TPU:32, one launch (start us, length us, event | category | flops | bytes accessed | tf_op | source)
XLA Modules:
  0.0 70.3 jit_solution(728522992864443740)
XLA Ops:
  1.9 1.3 %reshape.17.readout = bf16[1,512]{1,0:T(2,128)(2,1)} reshape(bf16[512]{0:T(512)(128)(2,1)} %param.21) | data formatting | bytes 2048 | tf_op jit(solution)/shard_map/reshape | solution.py:698
  3.2 64.7 %shard_map.157 = (bf16[256,512]{1,0:T(8,128)(2,1)}, bf16[32,2,32,128]{3,2,1,0:T(8,128)(2,1)}, s32[32,1,128]{2,1,0:T(1,128)}) custom-call(s32[1]{0:T(128)S(6)} %copy.17.parents, s32[1]{0:T(128)S(6)} %copy.18.visits, s32[32]{0:T(128)} %lengths.1, f32[1,128]{1,0:T(1,128)} %constant.2.clone.freq, bf16[256,512]{1,0:T(8,128)(2,1)} %hid.1, bf16[256,512]{1,0:T(8,128)(2,1)} %upper.1, ...), custom_call_target="tpu_custom_call" | custom-call | tf_op jit(solution)/shard_map/pallas_call | solution.py:670
  67.9 2.4 %shard_map.158 = (bf16[256,512]{1,0:T(8,128)(2,1)}, bf16[32,32,128]{2,1,0:T(8,128)(2,1)}, bf16[32,32,128]{2,1,0:T(8,128)(2,1)}) custom-call(s32[32,1,128]{2,1,0:T(1,128)} %get-tuple-element.6.par, bf16[32,2,32,128]{3,2,1,0:T(8,128)(2,1)} %get-tuple-element.7.got, bf16[256,512]{1,0:T(8,128)(2,1)} %get-tuple-element.8.gh_in), custom_call_target="tpu_custom_call" | custom-call | tf_op jit(solution)/shard_map/pallas_call | solution.py:703

commit v2 on v1

v2 whole, which is shorter than its diff:
```python
import functools

import jax
import jax.numpy as jnp
import numpy as np
from jax import lax
from jax.experimental import pallas as pl
from jax.experimental.pallas import tpu as pltpu
from jax.sharding import PartitionSpec as P

HEAD_SIZE = 128
GROUP = 4
EPS = 1e-06
ROPE_BASE = 1000000.0
LOSS_SCALE = 8192.0
SCALE = HEAD_SIZE ** (-0.5)
BF16 = jnp.bfloat16
F32 = jnp.float32


def dot_nn(a, b):
    return lax.dot_general(a, b, (((1,), (0,)), ((), ())), preferred_element_type=F32)


def dot_nt(a, b):
    return lax.dot_general(a, b, (((1,), (1,)), ((), ())), preferred_element_type=F32)


def dot_tn(a, b):
    return lax.dot_general(a, b, (((0,), (0,)), ((), ())), preferred_element_type=F32)


def slot_offsets(nz, ny):
    order = [0]
    for step in range(1, nz // 2 + 1):
        order.append(step)
        if len(order) < nz:
            order.append(-step)
    return [(dz, dy) for dz in order for dy in range(ny)]


def main_kernel(
    ny,
    parents,
    visits,
    lengths,
    freq,
    hid,
    upper,
    wq,
    wk,
    wv,
    qgain,
    kgain,
    readout,
    ck,
    cv,
    gh_out,
    dk_out,
    dv_out,
    cw_out,
    par_out,
    w,
    wsib,
    hf,
    cks,
    cvs,
    up,
    ue,
    par,
    par_s,
    hot,
    seen,
    kvs,
    kvf,
    acc,
    cosb,
    sinb,
    q,
    own,
    e,
    uv,
    rv,
    lsum,
    asum,
    bsum,
    tops,
    dv,
    gl,
    sch,
    sls,
    scl,
    dvs,
    dvr,
    dks,
    dkr,
    gx,
    gxr,
    gg,
    ps,
    rs_s,
    rs_r,
    in_sem,
    par_send,
    par_recv,
    s_sem,
    kv_send,
    kv_recv,
    ag_send,
    ag_recv,
    ws_send,
    ws_recv,
    sch_send,
    sch_recv,
    scl_send,
    scl_recv,
    dv_send,
    dv_recv,
    dk_send,
    dk_recv,
    gx_send,
    gx_recv,
    rs_send,
    rs_recv,
):
    me_l = lax.axis_index("leaf")
    me_g = lax.axis_index("head")
    nl = lax.axis_size("leaf")
    ng = lax.axis_size("head")
    nz = nl // ny
    nx = ng // 2
    z, y = me_l // ny, me_l % ny
    x, core = me_g // 2, me_g % 2
    nodes, rows, width = ck.shape
    tokens, feats = hid.shape
    half = tokens // 2
    offsets = slot_offsets(nz, ny)
    place = {(dz % nz, dy): slot for slot, (dz, dy) in enumerate(offsets)}
    mirror = [place[(-dz % nz, -dy % ny)] for dz, dy in offsets]
    per = 2 * ny
    chunks = nl // per

    def chip(dx, other=False):
        side = 1 - core if other else core
        return ((x + dx + nx) % nx) * 2 + side

    def leaf_of(slot):
        dz, dy = offsets[slot]
        return ((z + dz + nz) % nz) * ny + (y + dy) % ny

    def remote(src, dst, send, recv, **target):
        return pltpu.make_async_remote_copy(
            src_ref=src,
            dst_ref=dst,
            send_sem=send,
            recv_sem=recv,
            device_id=target,
            device_id_type=pl.DeviceIdType.MESH,
        )

    loads = [
        pltpu.make_async_copy(hid, hf.at[me_g], in_sem.at[0]),
        pltpu.make_async_copy(ck, cks, in_sem.at[1]),
        pltpu.make_async_copy(cv, cvs, in_sem.at[2]),
        pltpu.make_async_copy(wq, w.at[:, pl.ds(0, GROUP * width)], in_sem.at[3]),
        pltpu.make_async_copy(wk, w.at[:, pl.ds(GROUP * width, width)], in_sem.at[4]),
        pltpu.make_async_copy(wv, w.at[:, pl.ds((GROUP + 1) * width, width)], in_sem.at[5]),
        pltpu.make_async_copy(upper, up, in_sem.at[6]),
    ]
    for load in loads:
        load.start()

    barrier = pltpu.get_barrier_semaphore()
    for o in range(1, nl):
        pl.semaphore_signal(
            barrier, inc=1, device_id={"leaf": (me_l + o) % nl}, device_id_type=pl.DeviceIdType.MESH
        )
    for o in range(1, ng):
        pl.semaphore_signal(
            barrier, inc=1, device_id={"head": (me_g + o) % ng}, device_id_type=pl.DeviceIdType.MESH
        )
    lane = lax.broadcasted_iota(jnp.int32, (1, 128), 1)
    par[pl.ds(me_l, 1)] = jnp.where(lane == 0, parents[0], visits[0]).reshape(1, 1, 128)
    pl.semaphore_wait(barrier, nl - 1 + ng - 1)

    for o in range(1, nl):
        remote(
            par.at[me_l], par.at[me_l], par_send, par_recv, leaf=(me_l + o) % nl
        ).start()

    loads[0].wait()

    def ag_copy(sem, block, part, target):
        rows_at = hf.at[block, pl.ds(part * half, half)]
        return remote(rows_at, rows_at, ag_send.at[sem], ag_recv.at[block, part], head=target)

    def ag_wait(block, part):
        rows_at = hf.at[block, pl.ds(part * half, half)]
        remote(rows_at, rows_at, ag_send.at[0], ag_recv.at[block, part], head=me_g).wait_recv()

    right, left, sibling = chip(1), chip(-1), chip(0, True)
    ag = [
        ag_copy(0, me_g, 0, right),
        ag_copy(1, me_g, 1, left),
        ag_copy(2, me_g, 1, right),
        ag_copy(3, me_g, 0, left),
        ag_copy(4, me_g, 0, sibling),
        ag_copy(5, me_g, 1, sibling),
    ]
    for copy in ag:
        copy.start()

    loads[1].wait()
    loads[2].wait()
    some = par.at[pl.ds(0, nl - 1)]
    remote(some, some, par_send, par_recv, leaf=me_l).wait_recv()
    to_smem = pltpu.make_async_copy(par, par_s, s_sem)
    to_smem.start()
    to_smem.wait()
    for slot in range(nl):
        there = mirror[slot]
        dest = leaf_of(there)
        node = par_s[dest, 0, 0]
        if slot == 0:
            kvf[0, 0] = cks[node]
            kvf[0, 1] = cvs[node]
        else:
            kvs[slot, 0] = cks[node]
            kvs[slot, 1] = cvs[node]
            remote(
                kvs.at[slot], kvf.at[slot], kv_send, kv_recv.at[slot // per], leaf=dest
            ).start()

    for slot in range(nl):
        src = leaf_of(slot)
        par_out[slot] = jnp.full((1, 128), par_s[src, 0, 0], jnp.int32)
        hot[slot] = jnp.where((lane == par_s[src, 0, 0]) & (lane < nodes), 1.0, 0.0)
        seen[slot] = jnp.full((1, 128), par_s[src, 0, 1], jnp.int32).astype(F32)

    length = lengths[parents[0]]
    position = (length + lax.broadcasted_iota(jnp.int32, (tokens, width), 0)).astype(F32)
    angle = position * freq[...]
    cosb[...] = jnp.cos(angle)
    low = lax.broadcasted_iota(jnp.int32, (tokens, width), 1) < width // 2
    sine = jnp.sin(angle)
    sinb[...] = jnp.where(low, -sine, sine)

    def rotate(value):
        return value * cosb[...] + pltpu.roll(value, width // 2, 1) * sinb[...]

    def rotate_back(value):
        return value * cosb[...] - pltpu.roll(value, width // 2, 1) * sinb[...]

    loads[6].wait()
    at_lane = lax.broadcasted_iota(jnp.int32, (tokens, width), 1)
    for h in range(GROUP):
        ue[h, :, 0:width] = up[:, h * width : (h + 1) * width]
        ue[h, :, width : 2 * width] = jnp.where(at_lane == h, 1.0, 0.0).astype(BF16)
    read = [readout[h * width : (h + 1) * width].astype(F32).reshape(1, width) for h in range(GROUP)]
    read_rows = jnp.concatenate(read + [jnp.zeros((16 - GROUP, width), F32)], 0).astype(BF16)

    for i in (3, 4, 5):
        loads[i].wait()

    def block_rows(block):
        return pl.ds(pl.multiple_of(block * feats, feats), feats)

    def project(block, first=False):
        part = dot_nn(hf[block], w[block_rows(block), :])
        if first:
            acc[...] = part
        else:
            acc[...] += part

    def keys_of(i, which=0):
        if i == chunks:
            return own[which]
        return kvf[pl.ds(i * per, per), which].reshape(per * rows, width)

    def wait_rows(i):
        skip = 1 if i == 0 else 0
        some = kvf.at[pl.ds(i * per + skip, per - skip)]
        remote(some, some, kv_send, kv_recv.at[i], leaf=me_l).wait_recv()

    def values_product(i):
        values = keys_of(i, 1)
        for h in range(GROUP):
            uv[i, h] = dot_nt(values, up[:, h * width : (h + 1) * width])
        rv[i] = dot_nt(values, read_rows)

    project(me_g, True)

    def pass_on(*copies):
        for copy in copies:
            copy.start()
            ag.append(copy)

    ag_wait(left, 0)
    pass_on(ag_copy(6, left, 0, right), ag_copy(7, left, 0, sibling))
    ag_wait(right, 1)
    pass_on(ag_copy(8, right, 1, left), ag_copy(9, right, 1, sibling))
    ag_wait(sibling, 0)
    ag_wait(sibling, 1)
    project(sibling)
    ag_wait(left, 1)
    ag_wait(right, 0)
    pass_on(ag_copy(10, left, 1, sibling), ag_copy(11, right, 0, sibling))
    project(left)
    project(right)

    def project_other(dx):
        block = chip(dx, True)
        ag_wait(block, 0)
        ag_wait(block, 1)
        project(block)

    project_other(-1)
    project_other(1)
    wait_rows(0)
    values_product(0)
    opposite = chip(2)
    ag_wait(opposite, 0)
    pass_on(ag_copy(12, opposite, 0, sibling))
    ag_wait(opposite, 1)
    pass_on(ag_copy(13, opposite, 1, sibling))
    project(opposite)
    project_other(2)

    hops = (2, 1, -1, 0)
    ws_copies = []
    for j, dx in enumerate(hops):
        copy = remote(
            w.at[block_rows(chip(dx, True))], wsib.at[j], ws_send.at[j], ws_recv.at[j], head=sibling
        )
        copy.start()
        ws_copies.append(copy)

    def norm_inverse(raw):
        return lax.rsqrt(jnp.mean(raw * raw, axis=-1, keepdims=True) + EPS)

    for h in range(GROUP + 1):
        raw = acc[:, h * width : (h + 1) * width]
        gain = qgain[...] if h < GROUP else kgain[...]
        turned = rotate(raw * norm_inverse(raw) * gain).astype(BF16)
        if h < GROUP:
            q[h] = turned
        else:
            own[0] = turned
    own[1] = acc[:, (GROUP + 1) * width :].astype(BF16)

    def forward(i, first):
        keys = keys_of(i)
        if i == chunks:
            shape = (tokens, tokens)
            mask = lax.broadcasted_iota(jnp.int32, shape, 0) <= lax.broadcasted_iota(
                jnp.int32, shape, 1
            )
        else:
            at = lax.broadcasted_iota(jnp.int32, (rows, tokens), 0)
            mask = (
                jnp.concatenate([at + leaf_of(i * per + b) * rows for b in range(per)], 0) < length
            )
        for h in range(GROUP):
            logits = jnp.where(mask, dot_nt(keys, q[h]) * SCALE, -1e30)
            top = jnp.max(logits, axis=0, keepdims=True)
            if not first:
                before = tops[i_last[0], h : h + 1, :]
                top = jnp.maximum(top, before)
            weight = jnp.exp(logits - top)
            total = jnp.sum(weight, axis=0, keepdims=True)
            a = jnp.sum(weight * rv[i][:, h : h + 1], axis=0, keepdims=True)
            if not first:
                fade = jnp.exp(before - top)
                total += lsum[h : h + 1, :] * fade
                a += asum[h : h + 1, :] * fade
            lsum[h : h + 1, :] = total
            asum[h : h + 1, :] = a
            tops[i, h : h + 1, :] = top
            e[i, h] = weight
        i_last[0] = i

    i_last = [None]
    values_product(chunks)
    forward(chunks, True)
    forward(0, False)
    for i in range(1, chunks):
        wait_rows(i)
        values_product(i)
        forward(i, False)

    score = jnp.zeros((1, 1), F32)
    for h in range(GROUP):
        inverse = 1.0 / lsum[h : h + 1, :]
        lsum[h : h + 1, :] = inverse
        a = asum[h : h + 1, :] * inverse
        asum[h : h + 1, :] = a
        score += jnp.sum(a, axis=1, keepdims=True)
    sch[0] = jnp.broadcast_to(score / tokens, (1, 128))
    for o in range(1, ng):
        remote(sch.at[0], sch.at[o], sch_send, sch_recv, head=(me_g + o) % ng).start()

    for h in range(GROUP):
        b = jnp.zeros((1, tokens), F32)
        for i in range(chunks + 1):
            factor = lsum[h : h + 1, :]
            if i != chunks - 1:
                factor *= jnp.exp(tops[i, h : h + 1, :] - tops[chunks - 1, h : h + 1, :])
            prob = e[i, h] * factor
            e[i, h] = prob
            b += jnp.sum(prob * uv[i, h], axis=0, keepdims=True)
            term = dot_nn(prob.astype(BF16), ue[h])
            if h == 0:
                dv[i] = term
            else:
                dv[i] += term
        bsum[h : h + 1, :] = b

    def send_rows(buffer, target, send, recv, slot):
        remote(buffer.at[slot], target.at[mirror[slot]], send, recv, leaf=leaf_of(slot)).start()

    def send_values(i):
        dvs[pl.ds(i * per, per)] = dv[i][:, :width].astype(BF16).reshape(per, rows, width)
        for slot in range(i * per, (i + 1) * per):
            if slot == 0:
                dvr[0] = dvs[0]
            else:
                send_rows(dvs, dvr, dv_send, dv_recv, slot)

    for i in range(chunks // 2):
        send_values(i)

    parts = 128 // rows
    group = lane // rows
    diagonal = lax.broadcasted_iota(jnp.int32, (8, 128), 0) == lax.broadcasted_iota(
        jnp.int32, (8, 128), 1
    ) // rows
    for i in range(chunks):
        sums = dv[i][:, width:].T[0:8]
        for j in range(per // parts):
            tile = sums[:, j * 128 : (j + 1) * 128]
            turns = []
            for k in range(parts):
                moved = tile if k == 0 else pltpu.roll(tile, rows * k, 1)
                turns.append(jnp.sum(jnp.where(diagonal, moved, 0.0), axis=0, keepdims=True))
            for b in range(parts):
                line = turns[(0 - b) % parts]
                for h in range(1, parts):
                    line = jnp.where(group == h, turns[(h - b) % parts], line)
                sls[i * per + j * parts + b, 1:2] = line

    def norm_back(raw, gain, grad):
        inverse = norm_inverse(raw)
        scaled = grad * gain
        mean = jnp.mean(raw * scaled, axis=-1, keepdims=True)
        return (inverse * scaled - raw * (inverse * inverse * inverse) * mean).astype(BF16)

    gx_copies = [
        remote(gx.at[j], gxr.at[j], gx_send.at[j], gx_recv.at[j], head=sibling)
        for j in range(GROUP + 2)
    ]

    def query_grads(h):
        for part in range(2):
            back = None
            for i in range(chunks + 1):
                prob = e[i, h] * SCALE
                if part == 0:
                    grad = uv[i, h] - bsum[h : h + 1, :]
                else:
                    grad = rv[i][:, h : h + 1] - asum[h : h + 1, :]
                grad = (prob * grad).astype(BF16)
                gl[part, i, h] = grad
                term = dot_tn(keys_of(i), grad)
                back = term if back is None else back + term
            gx[h, part] = norm_back(
                acc[:, h * width : (h + 1) * width], qgain[...], rotate_back(back.T)
            )
        gx_copies[h].start()

    query_grads(0)

    some = sch.at[pl.ds(1, ng - 1)]
    remote(some, some, sch_send, sch_recv, head=me_g).wait_recv()
    step_score = jnp.sum(sch[...], axis=0)
    for slot in range(nl):
        sls[slot, 0:1] = step_score
    scl[0] = sls[0]
    for slot in range(1, nl):
        send_rows(sls, scl, scl_send, scl_recv, slot)
    for i in range(chunks // 2, chunks):
        send_values(i)
    for h in range(1, GROUP):
        query_grads(h)

    read_value = None
    for h in range(GROUP):
        term = dv[chunks][:, width + h : width + h + 1] * read[h]
        read_value = term if read_value is None else read_value + term
    gx[GROUP + 1, 0] = dv[chunks][:, :width].astype(BF16)
    gx[GROUP + 1, 1] = read_value.astype(BF16)
    gx_copies[GROUP + 1].start()
    for part in range(2):
        back = None
        for h in range(GROUP):
            term = dot_nn(gl[part, chunks, h], q[h])
            back = term if back is None else back + term
        cols = slice(GROUP * width, (GROUP + 1) * width)
        gx[GROUP, part] = norm_back(acc[:, cols], kgain[...], rotate_back(back))
    gx_copies[GROUP].start()

    some = scl.at[pl.ds(1, nl - 1)]
    remote(some, some, scl_send, scl_recv, leaf=me_l).wait_recv()
    match = hot[...]
    grown = jnp.exp(scl[:, 0:1, :])
    count = seen[...]
    node_total = jnp.sum(match * grown, axis=0, keepdims=True)
    node_seen = jnp.sum(match * count, axis=0, keepdims=True)
    total = jnp.sum(match * node_total, axis=2, keepdims=True)
    total_seen = jnp.sum(match * node_seen, axis=2, keepdims=True)
    scales = (LOSS_SCALE / tokens) * (grown / total - count / total_seen)
    cw_out[...] = scales * scl[:, 1:2, :]
    scale = scales[0, :, 0:1]

    for j in range(GROUP + 2):
        cols = slice(j * width, (j + 1) * width)
        gg[0, :, cols] = (gx[j, 0].astype(F32) + scale * gx[j, 1].astype(F32)).astype(BF16)
    for j in range(GROUP + 2):
        cols = slice(j * width, (j + 1) * width)
        gx_copies[j].wait_recv()
        gg[1, :, cols] = (gxr[j, 0].astype(F32) + scale * gxr[j, 1].astype(F32)).astype(BF16)

    def term(j):
        ws_copies[j].wait_recv()
        ps[j] = dot_nt(gg[0], w[block_rows(chip(hops[j])), :]) + dot_nt(gg[1], wsib[j])

    rs_copies = []

    def rs_send_rows(value, target):
        slot = len(rs_copies)
        rs_s[slot] = value.astype(BF16)
        copy = remote(
            rs_s.at[slot], rs_r.at[slot], rs_send.at[slot], rs_recv.at[slot], head=target
        )
        copy.start()
        rs_copies.append(copy)

    first, second = slice(0, half), slice(half, tokens)
    term(0)
    rs_send_rows(ps[0, first], right)
    rs_send_rows(ps[0, second], left)

    def send_keys(i):
        total = None
        for h in range(GROUP):
            grad = gl[0, i, h].astype(F32) + scale * gl[1, i, h].astype(F32)
            part = dot_nn(grad.astype(BF16), q[h])
            total = part if total is None else total + part
        dks[pl.ds(i * per, per)] = total.astype(BF16).reshape(per, rows, width)
        for slot in range(i * per, (i + 1) * per):
            if slot == 0:
                dkr[0] = dks[0]
            else:
                send_rows(dks, dkr, dk_send, dk_recv, slot)

    for i in range(chunks // 2):
        send_keys(i)
    term(1)
    rs_send_rows(ps[1, second], right)
    term(2)
    rs_send_rows(ps[2, first], left)
    for i in range(chunks // 2, chunks):
        send_keys(i)
    rs_copies[0].wait_recv()
    rs_send_rows(ps[1, first] + rs_r[0].astype(F32), right)
    rs_copies[1].wait_recv()
    rs_send_rows(ps[2, second] + rs_r[1].astype(F32), left)
    term(3)

    some = dvr.at[pl.ds(1, nl - 1)]
    remote(some, some, dv_send, dv_recv, leaf=me_l).wait_recv()
    dv_out[...] = dvr[...]
    remote(some, some, dk_send, dk_recv, leaf=me_l).wait_recv()
    dk_out[...] = dkr[...]

    for slot in range(2, 6):
        rs_copies[slot].wait_recv()
    gh_out[first, :] = (ps[3, first] + rs_r[4].astype(F32) + rs_r[3].astype(F32)).astype(BF16)
    gh_out[second, :] = (ps[3, second] + rs_r[2].astype(F32) + rs_r[5].astype(F32)).astype(BF16)

    for copy in ag + ws_copies + gx_copies + rs_copies:
        copy.wait_send()
    for buffer, send, recv in (
        (par, par_send, par_recv),
        (kvs, kv_send, kv_recv.at[0]),
        (dvs, dv_send, dv_recv),
        (dks, dk_send, dk_recv),
        (sls, scl_send, scl_recv),
    ):
        some = buffer.at[pl.ds(0, nl - 1)]
        remote(some, some, send, recv, leaf=me_l).wait_send()
    some = sch.at[pl.ds(1, ng - 1)]
    remote(some, some, sch_send, sch_recv, head=me_g).wait_send()


def collect_kernel(par, readout, dk_in, dv_in, cw, gh_in, gh, gk, gv, key_total, value_total, sums):
    nodes, rows, width = gk.shape
    key_total[...] = jnp.zeros_like(key_total)
    value_total[...] = jnp.zeros_like(value_total)
    sums[...] = jnp.zeros_like(sums)

    def add(s, c):
        node = par[s, 0, 0]
        key_total[node] += dk_in[s].astype(F32)
        value_total[node] += dv_in[s].astype(F32)
        sums[node] += cw[s]
        return c

    lax.fori_loop(0, dk_in.shape[0], add, 0)
    gk[...] = key_total[...].astype(BF16)
    shape = (1, rows, 128)
    keep = lax.broadcasted_iota(jnp.int32, shape, 2) % rows == lax.broadcasted_iota(
        jnp.int32, shape, 1
    )
    left = jnp.where(keep, sums[...], 0.0).reshape(nodes * rows, 128)
    high = left.astype(BF16)
    rest = (left - high.astype(F32)).astype(BF16)
    right = jnp.concatenate(
        [
            jnp.broadcast_to(
                readout[h * width : (h + 1) * width].astype(F32).reshape(1, width), (rows, width)
            )
            for h in range(128 // rows)
        ],
        0,
    ).astype(BF16)
    extra = dot_nn(high, right) + dot_nn(rest, right)
    gv[...] = (value_total[...] + extra.reshape(nodes, rows, width)).astype(BF16)
    gh[...] = gh_in[...]


def per_device(
    ny,
    hidden_states,
    upper_gradient,
    w_query,
    key_projection,
    value_projection,
    query_gain,
    key_norm_gain,
    readout,
    cached_prefix_keys,
    cached_prefix_values,
    prefix_lengths,
    parents,
    visits,
):
    nl, ng = lax.axis_size("leaf"), lax.axis_size("head")
    nodes, rows, width = cached_prefix_keys.shape
    tokens, feats = hidden_states.shape
    model = w_query.shape[0]
    blocks = nl // (2 * ny) + 1
    span = max(2 * ny * rows, tokens)
    half = tokens // 2
    cols = (GROUP + 2) * width
    inverse = np.asarray(
        ROPE_BASE ** (-2.0 * (np.arange(width) % (width // 2)) / width), np.float32
    ).reshape(1, width)
    smem = pl.BlockSpec(memory_space=pltpu.SMEM)
    vmem = pl.BlockSpec(memory_space=pltpu.VMEM)
    anywhere = pl.BlockSpec(memory_space=pl.ANY)
    dma = pltpu.SemaphoreType.DMA
    rows_of_all = pltpu.VMEM((nl, rows, width), BF16)
    scratch = [
        pltpu.VMEM((model, cols), BF16),
        pltpu.VMEM((4, feats, cols), BF16),
        pltpu.VMEM((ng, tokens, feats), BF16),
        pltpu.VMEM((nodes, rows, width), BF16),
        pltpu.VMEM((nodes, rows, width), BF16),
        pltpu.VMEM((tokens, GROUP * width), BF16),
        pltpu.VMEM((GROUP, tokens, 2 * width), BF16),
        pltpu.VMEM((nl, 1, 128), jnp.int32),
        pltpu.SMEM((nl, 1, 128), jnp.int32),
        pltpu.VMEM((nl, 1, 128), F32),
        pltpu.VMEM((nl, 1, 128), F32),
        pltpu.VMEM((nl, 2, rows, width), BF16),
        pltpu.VMEM((nl, 2, rows, width), BF16),
        pltpu.VMEM((tokens, cols), F32),
        pltpu.VMEM((tokens, width), F32),
        pltpu.VMEM((tokens, width), F32),
        pltpu.VMEM((GROUP, tokens, width), BF16),
        pltpu.VMEM((2, tokens, width), BF16),
        pltpu.VMEM((blocks, GROUP, span, tokens), F32),
        pltpu.VMEM((blocks, GROUP, span, tokens), F32),
        pltpu.VMEM((blocks, span, 16), F32),
        pltpu.VMEM((GROUP, tokens), F32),
        pltpu.VMEM((GROUP, tokens), F32),
        pltpu.VMEM((GROUP, tokens), F32),
        pltpu.VMEM((blocks, GROUP, tokens), F32),
        pltpu.VMEM((blocks, span, 2 * width), F32),
        pltpu.VMEM((2, blocks, GROUP, span, tokens), BF16),
        pltpu.VMEM((ng, 1, 128), F32),
        pltpu.VMEM((nl, 2, 128), F32),
        pltpu.VMEM((nl, 2, 128), F32),
        rows_of_all,
        rows_of_all,
        rows_of_all,
        rows_of_all,
        pltpu.VMEM((GROUP + 2, 2, tokens, width), BF16),
        pltpu.VMEM((GROUP + 2, 2, tokens, width), BF16),
        pltpu.VMEM((2, tokens, cols), BF16),
        pltpu.VMEM((4, tokens, feats), F32),
        pltpu.VMEM((6, half, feats), BF16),
        pltpu.VMEM((6, half, feats), BF16),
        dma((7,)),
        dma,
        dma,
        dma,
        dma,
        dma((blocks - 1,)),
        dma((14,)),
        dma((ng, 2)),
        dma((4,)),
        dma((4,)),
        dma,
        dma,
        dma,
        dma,
        dma,
        dma,
        dma,
        dma,
        dma((GROUP + 2,)),
        dma((GROUP + 2,)),
        dma((6,)),
        dma((6,)),
    ]
    table = jax.ShapeDtypeStruct((nodes, rows, width), BF16)
    per_slot = jax.ShapeDtypeStruct((nl, rows, width), BF16)
    grad_hidden = jax.ShapeDtypeStruct((tokens, feats), BF16)
    gh, dk, dv, cw, par = pl.pallas_call(
        functools.partial(main_kernel, ny),
        out_shape=(
            grad_hidden,
            per_slot,
            per_slot,
            jax.ShapeDtypeStruct((nl, 1, 128), F32),
            jax.ShapeDtypeStruct((nl, 1, 128), jnp.int32),
        ),
        in_specs=[smem, smem, smem, vmem] + [anywhere] * 5 + [vmem] * 3 + [anywhere] * 2,
        out_specs=(vmem, vmem, vmem, vmem, vmem),
        scratch_shapes=scratch,
        compiler_params=pltpu.CompilerParams(
            collective_id=0, has_side_effects=True, vmem_limit_bytes=58 * 1024 * 1024
        ),
    )(
        parents,
        visits,
        prefix_lengths,
        jnp.asarray(inverse),
        hidden_states,
        upper_gradient,
        w_query,
        key_projection,
        value_projection,
        query_gain.reshape(1, width),
        key_norm_gain.reshape(1, width),
        readout,
        cached_prefix_keys,
        cached_prefix_values,
    )
    return pl.pallas_call(
        collect_kernel,
        out_shape=(grad_hidden, table, table),
        in_specs=[smem] + [vmem] * 5,
        out_specs=(vmem, vmem, vmem),
        scratch_shapes=[
            pltpu.VMEM((nodes, rows, width), F32),
            pltpu.VMEM((nodes, rows, width), F32),
            pltpu.VMEM((nodes, 1, 128), F32),
        ],
        compiler_params=pltpu.CompilerParams(vmem_limit_bytes=16 * 1024 * 1024),
    )(par, readout, dk, dv, cw, gh)


def solution(mesh):
    in_specs = (
        P("leaf", "head"),
        P("leaf", "head"),
        P(None, "head"),
        P(None, "head"),
        P(None, "head"),
        P(),
        P(),
        P("head"),
        P(None, "leaf", "head"),
        P(None, "leaf", "head"),
        P(),
        P("leaf"),
        P("leaf"),
    )
    out_specs = (P("leaf", "head"), P(None, "leaf", "head"), P(None, "leaf", "head"))
    ny = 4 if mesh.shape["leaf"] % 4 == 0 else 1
    return jax.shard_map(
        functools.partial(per_device, ny),
        mesh=mesh,
        in_specs=in_specs,
        out_specs=out_specs,
        check_vma=False,
    )
```

time: 70.5 us -> 66.7 us (0.946)
  the two profiles are of different devices: /device:TPU:32 before, /device:TPU:1 now
where the time goes in v2:
time: 66.7 us; the launch traced here: 66.4 us
  Pallas kernels  60.1 us (90%)
  local copies, waits for them, and re-layouts  4.28 us (6%)
  between operations  1.98 us (3%)
    pallas_call x1, Pallas kernels, per_device(): pl.pallas_call(functools.partial(main_kernel, ny), out_shape=(grad_hidden...  57.8 us
    unnamed x12, local copies, waits for them, and re-layouts  4.28 us
    pallas_call x1, Pallas kernels, per_device(): pl.pallas_call(collect_kernel, out_shape=(grad_hidden, table, table), in_...  2.29 us

profile of v2, /device:TPU:1, one launch (start us, length us, event | category | flops | bytes accessed | tf_op | source)
XLA Modules:
  0.0 66.4 jit_solution(17089873404677097084)
XLA Ops:
  0.6 0.0 copy-start.5
  1.9 57.8 %shard_map.157 = (bf16[256,512]{1,0:T(8,128)(2,1)}, bf16[32,32,128]{2,1,0:T(8,128)(2,1)}, bf16[32,32,128]{2,1,0:T(8,128)(2,1)}, f32[32,1,128]{2,1,0:T(1,128)}, s32[32,1,128]{2,1,0:T(1,128)}) custom-call(s32[1]{0:T(128)S(6)} %copy.17.parents, s32[1]{0:T(128)S(6)} %copy.18.visits, s32[32]{0:T(128)} %lengths.1, f32[1,128]{1,0:T(1,128)} %constant.2.clone.freq, ...), custom_call_target="tpu_custom_call" | custom-call | tf_op jit(solution)/shard_map/pallas_call | solution.py:740
  59.8 0.0 copy-done.5
  59.8 0.0 copy-start
  59.8 0.9 %copy-done = bf16[256,512]{1,0:T(8,128)(2,1)S(1)} copy-done((bf16[256,512]{1,0:T(8,128)(2,1)S(1)}, bf16[256,512]{1,0:T(8,128)(2,1)}, u32[]{:S(2)}) %copy-start) | copy-done | bytes 262168
  60.8 0.0 copy-start.1
  60.8 0.9 %copy-done.1 = bf16[32,32,128]{2,1,0:T(8,128)(2,1)S(1)} copy-done((bf16[32,32,128]{2,1,0:T(8,128)(2,1)S(1)}, bf16[32,32,128]{2,1,0:T(8,128)(2,1)}, u32[]{:S(2)}) %copy-start.1) | copy-done | bytes 262168
  61.7 0.0 copy-start.2
  61.7 0.9 %copy-done.2 = bf16[32,32,128]{2,1,0:T(8,128)(2,1)S(1)} copy-done((bf16[32,32,128]{2,1,0:T(8,128)(2,1)S(1)}, bf16[32,32,128]{2,1,0:T(8,128)(2,1)}, u32[]{:S(2)}) %copy-start.2) | copy-done | bytes 262168
  62.7 0.0 copy-start.3
  62.7 0.7 %copy-done.3 = f32[32,1,128]{2,1,0:T(1,128)S(1)} copy-done((f32[32,1,128]{2,1,0:T(1,128)S(1)}, f32[32,1,128]{2,1,0:T(1,128)}, u32[]{:S(2)}) %copy-start.3) | copy-done | bytes 16408
  63.4 0.0 copy-start.4
  63.4 0.7 %copy-done.4 = s32[32,1,128]{2,1,0:T(1,128)S(1)} copy-done((s32[32,1,128]{2,1,0:T(1,128)S(1)}, s32[32,1,128]{2,1,0:T(1,128)}, u32[]{:S(2)}) %copy-start.4) | copy-done | bytes 16408
  64.1 2.3 %shard_map.158 = (bf16[256,512]{1,0:T(8,128)(2,1)}, bf16[32,32,128]{2,1,0:T(8,128)(2,1)}, bf16[32,32,128]{2,1,0:T(8,128)(2,1)}) custom-call(s32[32,1,128]{2,1,0:T(1,128)S(1)} %copy-done.4, bf16[512]{0:T(512)(128)(2,1)S(1)} %copy-done.5, bf16[32,32,128]{2,1,0:T(8,128)(2,1)S(1)} %copy-done.1, bf16[32,32,128]{2,1,0:T(8,128)(2,1)S(1)} %copy-done.2, ...), custom_call_target="tpu_custom_call" | custom-call | tf_op jit(solution)/shard_map/pallas_call | solution.py:771
Async XLA Ops:
  0.6 59.2 %copy-start.5 = (bf16[512]{0:T(512)(128)(2,1)S(1)}, bf16[512]{0:T(512)(128)(2,1)}, u32[]{:S(2)}) copy-start(bf16[512]{0:T(512)(128)(2,1)} %readout.3) | copy-start | bytes 3076
  59.8 1.0 %copy-start = (bf16[256,512]{1,0:T(8,128)(2,1)S(1)}, bf16[256,512]{1,0:T(8,128)(2,1)}, u32[]{:S(2)}) copy-start(bf16[256,512]{1,0:T(8,128)(2,1)} %get-tuple-element.12.gh_in) | copy-start | bytes 786436
  60.8 0.9 %copy-start.1 = (bf16[32,32,128]{2,1,0:T(8,128)(2,1)S(1)}, bf16[32,32,128]{2,1,0:T(8,128)(2,1)}, u32[]{:S(2)}) copy-start(bf16[32,32,128]{2,1,0:T(8,128)(2,1)} %get-tuple-element.9.dk_in) | copy-start | bytes 786436
  61.7 0.9 %copy-start.2 = (bf16[32,32,128]{2,1,0:T(8,128)(2,1)S(1)}, bf16[32,32,128]{2,1,0:T(8,128)(2,1)}, u32[]{:S(2)}) copy-start(bf16[32,32,128]{2,1,0:T(8,128)(2,1)} %get-tuple-element.10.dv_in) | copy-start | bytes 786436
  62.7 0.7 %copy-start.3 = (f32[32,1,128]{2,1,0:T(1,128)S(1)}, f32[32,1,128]{2,1,0:T(1,128)}, u32[]{:S(2)}) copy-start(f32[32,1,128]{2,1,0:T(1,128)} %get-tuple-element.11.cw) | copy-start | bytes 49156
  63.4 0.7 %copy-start.4 = (s32[32,1,128]{2,1,0:T(1,128)S(1)}, s32[32,1,128]{2,1,0:T(1,128)}, u32[]{:S(2)}) copy-start(s32[32,1,128]{2,1,0:T(1,128)} %get-tuple-element.8.par) | copy-start | bytes 49156

commit v3 on v2

--- a/solution.py
+++ b/solution.py
@@ -14,6 +14,7 @@
 ROPE_BASE = 1000000.0
 LOSS_SCALE = 8192.0
 SCALE = HEAD_SIZE ** (-0.5)
+TILE = 64
 BF16 = jnp.bfloat16
 F32 = jnp.float32
 
@@ -44,15 +45,15 @@
     parents,
     visits,
     lengths,
-    freq,
+    freq_in,
     hid,
     upper,
     wq,
     wk,
     wv,
-    qgain,
-    kgain,
-    readout,
+    qgain_in,
+    kgain_in,
+    readout_in,
     ck,
     cv,
     gh_out,
@@ -60,6 +61,10 @@
     dv_out,
     cw_out,
     par_out,
+    freq,
+    qgain,
+    kgain,
+    readout,
     w,
     wsib,
     hf,
@@ -67,8 +72,12 @@
     cvs,
     up,
     ue,
+    own_parent,
+    own_visits,
     par,
-    par_s,
+    par_slots,
+    cw,
+    gh,
     hot,
     seen,
     kvs,
@@ -103,7 +112,7 @@
     in_sem,
     par_send,
     par_recv,
-    s_sem,
+    out_sem,
     kv_send,
     kv_recv,
     ag_send,
@@ -158,6 +167,15 @@
             device_id_type=pl.DeviceIdType.MESH,
         )
 
+    barrier = pltpu.get_barrier_semaphore()
+    for o in range(1, nl):
+        pl.semaphore_signal(
+            barrier, inc=1, device_id={"leaf": (me_l + o) % nl}, device_id_type=pl.DeviceIdType.MESH
+        )
+    for o in range(1, ng):
+        pl.semaphore_signal(
+            barrier, inc=1, device_id={"head": (me_g + o) % ng}, device_id_type=pl.DeviceIdType.MESH
+        )
     loads = [
         pltpu.make_async_copy(hid, hf.at[me_g], in_sem.at[0]),
         pltpu.make_async_copy(ck, cks, in_sem.at[1]),
@@ -167,25 +185,34 @@
         pltpu.make_async_copy(wv, w.at[:, pl.ds((GROUP + 1) * width, width)], in_sem.at[5]),
         pltpu.make_async_copy(upper, up, in_sem.at[6]),
     ]
-    for load in loads:
+    small_loads = [
+        pltpu.make_async_copy(freq_in, freq, in_sem.at[9]),
+        pltpu.make_async_copy(qgain_in, qgain, in_sem.at[10]),
+        pltpu.make_async_copy(kgain_in, kgain, in_sem.at[11]),
+        pltpu.make_async_copy(readout_in, readout, in_sem.at[12]),
+    ]
+    first_loads = [
+        pltpu.make_async_copy(parents, own_parent, in_sem.at[7]),
+        pltpu.make_async_copy(visits, own_visits, in_sem.at[8]),
+    ]
+    for load in first_loads + loads + small_loads:
         load.start()
 
-    barrier = pltpu.get_barrier_semaphore()
-    for o in range(1, nl):
-        pl.semaphore_signal(
-            barrier, inc=1, device_id={"leaf": (me_l + o) % nl}, device_id_type=pl.DeviceIdType.MESH
-        )
-    for o in range(1, ng):
-        pl.semaphore_signal(
-            barrier, inc=1, device_id={"head": (me_g + o) % ng}, device_id_type=pl.DeviceIdType.MESH
-        )
     lane = lax.broadcasted_iota(jnp.int32, (1, 128), 1)
-    par[pl.ds(me_l, 1)] = jnp.where(lane == 0, parents[0], visits[0]).reshape(1, 1, 128)
+    for load in first_loads:
+        load.wait()
+    parent = own_parent[0]
+    par[pl.ds(me_l, 1)] = jnp.where(lane == 0, parent, own_visits[0]).reshape(1, 1, 128)
     pl.semaphore_wait(barrier, nl - 1 + ng - 1)
 
-    for o in range(1, nl):
+    planes = [0] + [abs(dz) for dz, _ in offsets[ny::ny]]
+    for slot in range(1, nl):
         remote(
-            par.at[me_l], par.at[me_l], par_send, par_recv, leaf=(me_l + o) % nl
+            par.at[me_l],
+            par.at[me_l],
+            par_send,
+            par_recv.at[planes[slot // ny]],
+            leaf=leaf_of(slot),
         ).start()
 
     loads[0].wait()
@@ -212,32 +239,45 @@
 
     loads[1].wait()
     loads[2].wait()
-    some = par.at[pl.ds(0, nl - 1)]
-    remote(some, some, par_send, par_recv, leaf=me_l).wait_recv()
-    to_smem = pltpu.make_async_copy(par, par_s, s_sem)
-    to_smem.start()
-    to_smem.wait()
-    for slot in range(nl):
-        there = mirror[slot]
-        dest = leaf_of(there)
-        node = par_s[dest, 0, 0]
-        if slot == 0:
-            kvf[0, 0] = cks[node]
-            kvf[0, 1] = cvs[node]
-        else:
-            kvs[slot, 0] = cks[node]
-            kvs[slot, 1] = cvs[node]
-            remote(
-                kvs.at[slot], kvf.at[slot], kv_send, kv_recv.at[slot // per], leaf=dest
-            ).start()
+    for plane in range(nz // 2 + 1):
+        members = [slot for slot in range(nl) if planes[slot // ny] == plane]
+        some = par.at[pl.ds(0, len([slot for slot in members if slot > 0]))]
+        remote(some, some, par_send, par_recv.at[plane], leaf=me_l).wait_recv()
+        for slot in members:
+            dest = leaf_of(mirror[slot])
+            node = par[dest, 0, 0]
+            if slot == 0:
+                kvf[0, 0] = cks[node]
+                kvf[0, 1] = cvs[node]
+            else:
+                kvs[slot, 0] = cks[node]
+                kvs[slot, 1] = cvs[node]
+                remote(
+                    kvs.at[slot], kvf.at[slot], kv_send, kv_recv.at[slot // per], leaf=dest
+                ).start()
+
+    def pass_on(*copies):
+        for copy in copies:
+            copy.start()
+            ag.append(copy)
+
+    ag_wait(left, 0)
+    pass_on(ag_copy(6, left, 0, right), ag_copy(7, left, 0, sibling))
+    ag_wait(right, 1)
+    pass_on(ag_copy(8, right, 1, left), ag_copy(9, right, 1, sibling))
 
     for slot in range(nl):
         src = leaf_of(slot)
-        par_out[slot] = jnp.full((1, 128), par_s[src, 0, 0], jnp.int32)
-        hot[slot] = jnp.where((lane == par_s[src, 0, 0]) & (lane < nodes), 1.0, 0.0)
-        seen[slot] = jnp.full((1, 128), par_s[src, 0, 1], jnp.int32).astype(F32)
-
-    length = lengths[parents[0]]
+        par_row = jnp.full((1, 128), par[src, 0, 0], jnp.int32)
+        par_slots[slot] = par_row
+        hot[slot] = jnp.where((lane == par_row) & (lane < nodes), 1.0, 0.0)
+        seen[slot] = jnp.full((1, 128), par[src, 0, 1], jnp.int32).astype(F32)
+    outs = [pltpu.make_async_copy(par_slots, par_out, out_sem.at[0])]
+    outs[0].start()
+
+    for load in small_loads:
+        load.wait()
+    length = lengths[parent]
     position = (length + lax.broadcasted_iota(jnp.int32, (tokens, width), 0)).astype(F32)
     angle = position * freq[...]
     cosb[...] = jnp.cos(angle)
@@ -290,15 +330,6 @@
 
     project(me_g, True)
 
-    def pass_on(*copies):
-        for copy in copies:
-            copy.start()
-            ag.append(copy)
-
-    ag_wait(left, 0)
-    pass_on(ag_copy(6, left, 0, right), ag_copy(7, left, 0, sibling))
-    ag_wait(right, 1)
-    pass_on(ag_copy(8, right, 1, left), ag_copy(9, right, 1, sibling))
     ag_wait(sibling, 0)
     ag_wait(sibling, 1)
     project(sibling)
@@ -405,10 +436,13 @@
             factor = lsum[h : h + 1, :]
             if i != chunks - 1:
                 factor *= jnp.exp(tops[i, h : h + 1, :] - tops[chunks - 1, h : h + 1, :])
-            prob = e[i, h] * factor
-            e[i, h] = prob
-            b += jnp.sum(prob * uv[i, h], axis=0, keepdims=True)
-            term = dot_nn(prob.astype(BF16), ue[h])
+            for at in range(0, keys_of(i).shape[0], TILE):
+                tile = slice(at, at + TILE)
+                prob = e[i, h, tile] * factor
+                e[i, h, tile] = prob
+                gl[0, i, h, tile] = prob.astype(BF16)
+                b += jnp.sum(prob * uv[i, h, tile], axis=0, keepdims=True)
+            term = dot_nn(gl[0, i, h], ue[h])
             if h == 0:
                 dv[i] = term
             else:
@@ -425,9 +459,6 @@
                 dvr[0] = dvs[0]
             else:
                 send_rows(dvs, dvr, dv_send, dv_recv, slot)
-
-    for i in range(chunks // 2):
-        send_values(i)
 
     parts = 128 // rows
     group = lane // rows
@@ -460,24 +491,26 @@
     ]
 
     def query_grads(h):
+        back = [None, None]
+        for i in range(chunks + 1):
+            keys = keys_of(i)
+            for at in range(0, keys.shape[0], TILE):
+                tile = slice(at, at + TILE)
+                prob = e[i, h, tile] * SCALE
+                grad = prob * (uv[i, h, tile] - bsum[h : h + 1, :])
+                gl[0, i, h, tile] = grad.astype(BF16)
+                grad = prob * (rv[i, tile, h : h + 1] - asum[h : h + 1, :])
+                gl[1, i, h, tile] = grad.astype(BF16)
+            for part in range(2):
+                term = dot_tn(keys, gl[part, i, h])
+                back[part] = term if i == 0 else back[part] + term
+        raw = acc[:, h * width : (h + 1) * width]
         for part in range(2):
-            back = None
-            for i in range(chunks + 1):
-                prob = e[i, h] * SCALE
-                if part == 0:
-                    grad = uv[i, h] - bsum[h : h + 1, :]
-                else:
-                    grad = rv[i][:, h : h + 1] - asum[h : h + 1, :]
-                grad = (prob * grad).astype(BF16)
-                gl[part, i, h] = grad
-                term = dot_tn(keys_of(i), grad)
-                back = term if back is None else back + term
-            gx[h, part] = norm_back(
-                acc[:, h * width : (h + 1) * width], qgain[...], rotate_back(back.T)
-            )
+            gx[h, part] = norm_back(raw, qgain[...], rotate_back(back[part].T))
         gx_copies[h].start()
 
     query_grads(0)
+    query_grads(1)
 
     some = sch.at[pl.ds(1, ng - 1)]
     remote(some, some, sch_send, sch_recv, head=me_g).wait_recv()
@@ -487,9 +520,9 @@
     scl[0] = sls[0]
     for slot in range(1, nl):
         send_rows(sls, scl, scl_send, scl_recv, slot)
-    for i in range(chunks // 2, chunks):
+    for i in range(chunks):
         send_values(i)
-    for h in range(1, GROUP):
+    for h in range(2, GROUP):
         query_grads(h)
 
     read_value = None
@@ -518,7 +551,9 @@
     total = jnp.sum(match * node_total, axis=2, keepdims=True)
     total_seen = jnp.sum(match * node_seen, axis=2, keepdims=True)
     scales = (LOSS_SCALE / tokens) * (grown / total - count / total_seen)
-    cw_out[...] = scales * scl[:, 1:2, :]
+    cw[...] = scales * scl[:, 1:2, :]
+    outs.append(pltpu.make_async_copy(cw, cw_out, out_sem.at[1]))
+    outs[1].start()
     scale = scales[0, :, 0:1]
 
     for j in range(GROUP + 2):
@@ -552,8 +587,11 @@
     def send_keys(i):
         total = None
         for h in range(GROUP):
-            grad = gl[0, i, h].astype(F32) + scale * gl[1, i, h].astype(F32)
-            part = dot_nn(grad.astype(BF16), q[h])
+            for at in range(0, per * rows, TILE):
+                tile = slice(at, at + TILE)
+                grad = gl[0, i, h, tile].astype(F32) + scale * gl[1, i, h, tile].astype(F32)
+                gl[0, i, h, tile] = grad.astype(BF16)
+            part = dot_nn(gl[0, i, h], q[h])
             total = part if total is None else total + part
         dks[pl.ds(i * per, per)] = total.astype(BF16).reshape(per, rows, width)
         for slot in range(i * per, (i + 1) * per):
@@ -578,14 +616,19 @@
 
     some = dvr.at[pl.ds(1, nl - 1)]
     remote(some, some, dv_send, dv_recv, leaf=me_l).wait_recv()
-    dv_out[...] = dvr[...]
+    outs.append(pltpu.make_async_copy(dvr, dv_out, out_sem.at[2]))
+    outs[2].start()
     remote(some, some, dk_send, dk_recv, leaf=me_l).wait_recv()
-    dk_out[...] = dkr[...]
+    outs.append(pltpu.make_async_copy(dkr, dk_out, out_sem.at[3]))
+    outs[3].start()
 
     for slot in range(2, 6):
         rs_copies[slot].wait_recv()
-    gh_out[first, :] = (ps[3, first] + rs_r[4].astype(F32) + rs_r[3].astype(F32)).astype(BF16)
-    gh_out[second, :] = (ps[3, second] + rs_r[2].astype(F32) + rs_r[5].astype(F32)).astype(BF16)
+    gh[first, :] = (ps[3, first] + rs_r[4].astype(F32) + rs_r[3].astype(F32)).astype(BF16)
+    gh[second, :] = (ps[3, second] + rs_r[2].astype(F32) + rs_r[5].astype(F32)).astype(BF16)
+
+    outs.append(pltpu.make_async_copy(gh, gh_out, out_sem.at[4]))
+    outs[4].start()
 
     for copy in ag + ws_copies + gx_copies + rs_copies:
         copy.wait_send()
@@ -600,9 +643,11 @@
         remote(some, some, send, recv, leaf=me_l).wait_send()
     some = sch.at[pl.ds(1, ng - 1)]
     remote(some, some, sch_send, sch_recv, head=me_g).wait_send()
-
-
-def collect_kernel(par, readout, dk_in, dv_in, cw, gh_in, gh, gk, gv, key_total, value_total, sums):
+    for out in outs:
+        out.wait()
+
+
+def collect_kernel(par, readout, cw, dk_in, dv_in, gh_in, gh, gk, gv, key_total, value_total, sums):
     nodes, rows, width = gk.shape
     key_total[...] = jnp.zeros_like(key_total)
     value_total[...] = jnp.zeros_like(value_total)
@@ -615,7 +660,7 @@
         sums[node] += cw[s]
         return c
 
-    lax.fori_loop(0, dk_in.shape[0], add, 0)
+    lax.fori_loop(0, dk_in.shape[0], add, 0, unroll=4)
     gk[...] = key_total[...].astype(BF16)
     shape = (1, rows, 128)
     keep = lax.broadcasted_iota(jnp.int32, shape, 2) % rows == lax.broadcasted_iota(
@@ -668,9 +713,14 @@
     smem = pl.BlockSpec(memory_space=pltpu.SMEM)
     vmem = pl.BlockSpec(memory_space=pltpu.VMEM)
     anywhere = pl.BlockSpec(memory_space=pl.ANY)
+    hbm = pl.BlockSpec(memory_space=pltpu.HBM)
     dma = pltpu.SemaphoreType.DMA
     rows_of_all = pltpu.VMEM((nl, rows, width), BF16)
     scratch = [
+        pltpu.VMEM((1, width), F32),
+        pltpu.VMEM((1, width), F32),
+        pltpu.VMEM((1, width), F32),
+        pltpu.VMEM((GROUP * width,), BF16),
         pltpu.VMEM((model, cols), BF16),
         pltpu.VMEM((4, feats, cols), BF16),
         pltpu.VMEM((ng, tokens, feats), BF16),
@@ -678,8 +728,12 @@
         pltpu.VMEM((nodes, rows, width), BF16),
         pltpu.VMEM((tokens, GROUP * width), BF16),
         pltpu.VMEM((GROUP, tokens, 2 * width), BF16),
+        pltpu.VMEM((1,), jnp.int32),
+        pltpu.VMEM((1,), jnp.int32),
         pltpu.VMEM((nl, 1, 128), jnp.int32),
-        pltpu.SMEM((nl, 1, 128), jnp.int32),
+        pltpu.VMEM((nl, 1, 128), jnp.int32),
+        pltpu.VMEM((nl, 1, 128), F32),
+        pltpu.VMEM((tokens, feats), BF16),
         pltpu.VMEM((nl, 1, 128), F32),
         pltpu.VMEM((nl, 1, 128), F32),
         pltpu.VMEM((nl, 2, rows, width), BF16),
@@ -711,10 +765,10 @@
         pltpu.VMEM((4, tokens, feats), F32),
         pltpu.VMEM((6, half, feats), BF16),
         pltpu.VMEM((6, half, feats), BF16),
-        dma((7,)),
-        dma,
-        dma,
-        dma,
+        dma((13,)),
+        dma,
+        dma((blocks,)),
+        dma((5,)),
         dma,
         dma((blocks - 1,)),
         dma((14,)),
@@ -746,8 +800,8 @@
             jax.ShapeDtypeStruct((nl, 1, 128), F32),
             jax.ShapeDtypeStruct((nl, 1, 128), jnp.int32),
         ),
-        in_specs=[smem, smem, smem, vmem] + [anywhere] * 5 + [vmem] * 3 + [anywhere] * 2,
-        out_specs=(vmem, vmem, vmem, vmem, vmem),
+        in_specs=[hbm, hbm, smem, hbm] + [anywhere] * 5 + [hbm] * 3 + [anywhere] * 2,
+        out_specs=(anywhere,) * 5,
         scratch_shapes=scratch,
         compiler_params=pltpu.CompilerParams(
             collective_id=0, has_side_effects=True, vmem_limit_bytes=58 * 1024 * 1024
@@ -772,14 +826,14 @@
         collect_kernel,
         out_shape=(grad_hidden, table, table),
         in_specs=[smem] + [vmem] * 5,
-        out_specs=(vmem, vmem, vmem),
+        out_specs=(vmem,) * 3,
         scratch_shapes=[
             pltpu.VMEM((nodes, rows, width), F32),
             pltpu.VMEM((nodes, rows, width), F32),
             pltpu.VMEM((nodes, 1, 128), F32),
         ],
-        compiler_params=pltpu.CompilerParams(vmem_limit_bytes=16 * 1024 * 1024),
-    )(par, readout, dk, dv, cw, gh)
+        compiler_params=pltpu.CompilerParams(vmem_limit_bytes=58 * 1024 * 1024),
+    )(par, readout, cw, dk, dv, gh)
 
 
 def solution(mesh):

time: 66.7 us -> 57.9 us (0.87)
  the two profiles are of different devices: /device:TPU:1 before, /device:TPU:32 now
where the time goes in v3:
time: 57.9 us; the launch traced here: 57.7 us
  Pallas kernels  55.8 us (96%)
  between operations  1.93 us (3%)
    pallas_call x1, Pallas kernels, per_device(): pl.pallas_call(functools.partial(main_kernel, ny), out_shape=(grad_hidden...  53.2 us
    pallas_call x1, Pallas kernels, per_device(): pl.pallas_call(collect_kernel, out_shape=(grad_hidden, table, table), in_...  2.55 us

profile of v3, /device:TPU:32, one launch (start us, length us, event | category | flops | bytes accessed | tf_op | source)
XLA Modules:
  0.0 57.7 jit_solution(15418544903361219414)
XLA Ops:
  1.9 53.2 %shard_map.157 = (bf16[256,512]{1,0:T(8,128)(2,1)}, bf16[32,32,128]{2,1,0:T(8,128)(2,1)}, bf16[32,32,128]{2,1,0:T(8,128)(2,1)}, f32[32,1,128]{2,1,0:T(1,128)}, s32[32,1,128]{2,1,0:T(1,128)}) custom-call(s32[1]{0:T(128)S(6)} %copy.17.parents, s32[1]{0:T(128)S(6)} %copy.18.visits, s32[32]{0:T(128)} %lengths.1, f32[1,128]{1,0:T(1,128)} %constant.2.clone.freq_in, ...), custom_call_target="tpu_custom_call" | custom-call | tf_op jit(solution)/shard_map/pallas_call | solution.py:794
  55.2 2.6 %shard_map.158 = (bf16[256,512]{1,0:T(8,128)(2,1)}, bf16[32,32,128]{2,1,0:T(8,128)(2,1)}, bf16[32,32,128]{2,1,0:T(8,128)(2,1)}) custom-call(s32[32,1,128]{2,1,0:T(1,128)} %get-tuple-element.8.par, bf16[512]{0:T(512)(128)(2,1)} %readout.1, f32[32,1,128]{2,1,0:T(1,128)} %get-tuple-element.9.cw, bf16[32,32,128]{2,1,0:T(8,128)(2,1)} %get-tuple-element.10.dk_in, ...), custom_call_target="tpu_custom_call" | custom-call | tf_op jit(solution)/shard_map/pallas_call | solution.py:825

commit v4 on v3

--- a/solution.py
+++ b/solution.py
@@ -96,6 +96,7 @@
     tops,
     dv,
     gl,
+    dk,
     sch,
     sls,
     scl,
@@ -105,7 +106,9 @@
     dkr,
     gx,
     gxr,
+    gab,
     gg,
+    far,
     ps,
     rs_s,
     rs_r,
@@ -520,10 +523,12 @@
     scl[0] = sls[0]
     for slot in range(1, nl):
         send_rows(sls, scl, scl_send, scl_recv, slot)
-    for i in range(chunks):
+    for i in range(1):
         send_values(i)
-    for h in range(2, GROUP):
-        query_grads(h)
+    query_grads(2)
+    for i in range(1,4):
+        send_values(i)
+    query_grads(3)
 
     read_value = None
     for h in range(GROUP):
@@ -541,6 +546,28 @@
         gx[GROUP, part] = norm_back(acc[:, cols], kgain[...], rotate_back(back))
     gx_copies[GROUP].start()
 
+    for i in range(chunks):
+        for part in range(2):
+            total = None
+            for h in range(GROUP):
+                product = dot_nn(gl[part, i, h], q[h])
+                total = product if total is None else total + product
+            dk[part, i] = total
+    for j in range(GROUP + 2):
+        cols = slice(j * width, (j + 1) * width)
+        gx_copies[j].wait_recv()
+        for part in range(2):
+            gab[0, part, :, cols] = gx[j, part]
+            gab[1, part, :, cols] = gxr[j, part]
+
+    def term(left, j):
+        return dot_nt(left[0], w[block_rows(chip(hops[j])), :]) + dot_nt(left[1], wsib[j])
+
+    for copy in ws_copies:
+        copy.wait_recv()
+    for part in range(2):
+        far[part] = term([gab[0, part], gab[1, part]], 0)
+
     some = scl.at[pl.ds(1, nl - 1)]
     remote(some, some, scl_send, scl_recv, leaf=me_l).wait_recv()
     match = hot[...]
@@ -556,18 +583,6 @@
     outs[1].start()
     scale = scales[0, :, 0:1]
 
-    for j in range(GROUP + 2):
-        cols = slice(j * width, (j + 1) * width)
-        gg[0, :, cols] = (gx[j, 0].astype(F32) + scale * gx[j, 1].astype(F32)).astype(BF16)
-    for j in range(GROUP + 2):
-        cols = slice(j * width, (j + 1) * width)
-        gx_copies[j].wait_recv()
-        gg[1, :, cols] = (gxr[j, 0].astype(F32) + scale * gxr[j, 1].astype(F32)).astype(BF16)
-
-    def term(j):
-        ws_copies[j].wait_recv()
-        ps[j] = dot_nt(gg[0], w[block_rows(chip(hops[j])), :]) + dot_nt(gg[1], wsib[j])
-
     rs_copies = []
 
     def rs_send_rows(value, target):
@@ -580,19 +595,11 @@
         rs_copies.append(copy)
 
     first, second = slice(0, half), slice(half, tokens)
-    term(0)
-    rs_send_rows(ps[0, first], right)
-    rs_send_rows(ps[0, second], left)
+    rs_send_rows(far[0, first] + scale * far[1, first], right)
+    rs_send_rows(far[0, second] + scale * far[1, second], left)
 
     def send_keys(i):
-        total = None
-        for h in range(GROUP):
-            for at in range(0, per * rows, TILE):
-                tile = slice(at, at + TILE)
-                grad = gl[0, i, h, tile].astype(F32) + scale * gl[1, i, h, tile].astype(F32)
-                gl[0, i, h, tile] = grad.astype(BF16)
-            part = dot_nn(gl[0, i, h], q[h])
-            total = part if total is None else total + part
+        total = dk[0, i] + scale * dk[1, i]
         dks[pl.ds(i * per, per)] = total.astype(BF16).reshape(per, rows, width)
         for slot in range(i * per, (i + 1) * per):
             if slot == 0:
@@ -602,17 +609,22 @@
 
     for i in range(chunks // 2):
         send_keys(i)
-    term(1)
-    rs_send_rows(ps[1, second], right)
-    term(2)
-    rs_send_rows(ps[2, first], left)
+    for side in range(2):
+        for at in range(0, tokens, TILE):
+            tile = slice(at, at + TILE)
+            grad = gab[side, 0, tile].astype(F32) + scale * gab[side, 1, tile].astype(F32)
+            gg[side, tile] = grad.astype(BF16)
+    ps[0] = term(gg, 1)
+    rs_send_rows(ps[0, second], right)
+    ps[1] = term(gg, 2)
+    rs_send_rows(ps[1, first], left)
     for i in range(chunks // 2, chunks):
         send_keys(i)
     rs_copies[0].wait_recv()
-    rs_send_rows(ps[1, first] + rs_r[0].astype(F32), right)
+    rs_send_rows(ps[0, first] + rs_r[0].astype(F32), right)
     rs_copies[1].wait_recv()
-    rs_send_rows(ps[2, second] + rs_r[1].astype(F32), left)
-    term(3)
+    rs_send_rows(ps[1, second] + rs_r[1].astype(F32), left)
+    ps[2] = term(gg, 3)
 
     some = dvr.at[pl.ds(1, nl - 1)]
     remote(some, some, dv_send, dv_recv, leaf=me_l).wait_recv()
@@ -624,8 +636,8 @@
 
     for slot in range(2, 6):
         rs_copies[slot].wait_recv()
-    gh[first, :] = (ps[3, first] + rs_r[4].astype(F32) + rs_r[3].astype(F32)).astype(BF16)
-    gh[second, :] = (ps[3, second] + rs_r[2].astype(F32) + rs_r[5].astype(F32)).astype(BF16)
+    gh[first, :] = (ps[2, first] + rs_r[4].astype(F32) + rs_r[3].astype(F32)).astype(BF16)
+    gh[second, :] = (ps[2, second] + rs_r[2].astype(F32) + rs_r[5].astype(F32)).astype(BF16)
 
     outs.append(pltpu.make_async_copy(gh, gh_out, out_sem.at[4]))
     outs[4].start()
@@ -752,6 +764,7 @@
         pltpu.VMEM((blocks, GROUP, tokens), F32),
         pltpu.VMEM((blocks, span, 2 * width), F32),
         pltpu.VMEM((2, blocks, GROUP, span, tokens), BF16),
+        pltpu.VMEM((2, blocks - 1, 2 * ny * rows, width), F32),
         pltpu.VMEM((ng, 1, 128), F32),
         pltpu.VMEM((nl, 2, 128), F32),
         pltpu.VMEM((nl, 2, 128), F32),
@@ -761,8 +774,10 @@
         rows_of_all,
         pltpu.VMEM((GROUP + 2, 2, tokens, width), BF16),
         pltpu.VMEM((GROUP + 2, 2, tokens, width), BF16),
+        pltpu.VMEM((2, 2, tokens, cols), BF16),
         pltpu.VMEM((2, tokens, cols), BF16),
-        pltpu.VMEM((4, tokens, feats), F32),
+        pltpu.VMEM((2, tokens, feats), F32),
+        pltpu.VMEM((3, tokens, feats), F32),
         pltpu.VMEM((6, half, feats), BF16),
         pltpu.VMEM((6, half, feats), BF16),
         dma((13,)),

time: 57.9 us -> 56.3 us (0.972)
  Pallas kernels: 55.8 us -> 54.2 us
    pallas_call x1, Pallas kernels: 53.2 us -> 51.6 us  [per_device(): pl.pallas_call(functools.partial(main_kernel, ny), out_shape=(grad_hidden...]
where the time goes in v4:
time: 56.3 us; the launch traced here: 56.1 us
  Pallas kernels  54.2 us (96%)
  between operations  1.93 us (3%)
    pallas_call x1, Pallas kernels, per_device(): pl.pallas_call(functools.partial(main_kernel, ny), out_shape=(grad_hidden...  51.6 us
    pallas_call x1, Pallas kernels, per_device(): pl.pallas_call(collect_kernel, out_shape=(grad_hidden, table, table), in_...  2.55 us

profile of v4, /device:TPU:32, one launch (start us, length us, event | category | flops | bytes accessed | tf_op | source)
XLA Modules:
  0.0 56.1 jit_solution(12848371932203013855)
XLA Ops:
  1.9 51.6 %shard_map.157 = (bf16[256,512]{1,0:T(8,128)(2,1)}, bf16[32,32,128]{2,1,0:T(8,128)(2,1)}, bf16[32,32,128]{2,1,0:T(8,128)(2,1)}, f32[32,1,128]{2,1,0:T(1,128)}, s32[32,1,128]{2,1,0:T(1,128)}) custom-call(s32[1]{0:T(128)S(6)} %copy.17.parents, s32[1]{0:T(128)S(6)} %copy.18.visits, s32[32]{0:T(128)} %lengths.1, f32[1,128]{1,0:T(1,128)} %constant.2.clone.freq_in, ...), custom_call_target="tpu_custom_call" | custom-call | tf_op jit(solution)/shard_map/pallas_call | solution.py:809
  53.5 2.5 %shard_map.158 = (bf16[256,512]{1,0:T(8,128)(2,1)}, bf16[32,32,128]{2,1,0:T(8,128)(2,1)}, bf16[32,32,128]{2,1,0:T(8,128)(2,1)}) custom-call(s32[32,1,128]{2,1,0:T(1,128)} %get-tuple-element.8.par, bf16[512]{0:T(512)(128)(2,1)} %readout.1, f32[32,1,128]{2,1,0:T(1,128)} %get-tuple-element.9.cw, bf16[32,32,128]{2,1,0:T(8,128)(2,1)} %get-tuple-element.10.dk_in, ...), custom_call_target="tpu_custom_call" | custom-call | tf_op jit(solution)/shard_map/pallas_call | solution.py:840

commit v5 on v4

--- a/solution.py
+++ b/solution.py
@@ -58,8 +58,7 @@
     cv,
     gh_out,
     dk_out,
-    dv_out,
-    cw_out,
+    gv_out,
     par_out,
     freq,
     qgain,
@@ -104,6 +103,7 @@
     dvr,
     dks,
     dkr,
+    gvs,
     gx,
     gxr,
     gab,
@@ -171,9 +171,9 @@
         )
 
     barrier = pltpu.get_barrier_semaphore()
-    for o in range(1, nl):
+    for slot in reversed(range(1, nl)):
         pl.semaphore_signal(
-            barrier, inc=1, device_id={"leaf": (me_l + o) % nl}, device_id_type=pl.DeviceIdType.MESH
+            barrier, inc=1, device_id={"leaf": leaf_of(slot)}, device_id_type=pl.DeviceIdType.MESH
         )
     for o in range(1, ng):
         pl.semaphore_signal(
@@ -198,7 +198,7 @@
         pltpu.make_async_copy(parents, own_parent, in_sem.at[7]),
         pltpu.make_async_copy(visits, own_visits, in_sem.at[8]),
     ]
-    for load in first_loads + loads + small_loads:
+    for load in first_loads + loads[:3]:
         load.start()
 
     lane = lax.broadcasted_iota(jnp.int32, (1, 128), 1)
@@ -239,6 +239,8 @@
     ]
     for copy in ag:
         copy.start()
+    for load in loads[3:] + small_loads:
+        load.start()
 
     loads[1].wait()
     loads[2].wait()
@@ -521,7 +523,7 @@
     for slot in range(nl):
         sls[slot, 0:1] = step_score
     scl[0] = sls[0]
-    for slot in range(1, nl):
+    for slot in reversed(range(1, nl)):
         send_rows(sls, scl, scl_send, scl_recv, slot)
     for i in range(1):
         send_values(i)
@@ -579,8 +581,6 @@
     total_seen = jnp.sum(match * node_seen, axis=2, keepdims=True)
     scales = (LOSS_SCALE / tokens) * (grown / total - count / total_seen)
     cw[...] = scales * scl[:, 1:2, :]
-    outs.append(pltpu.make_async_copy(cw, cw_out, out_sem.at[1]))
-    outs[1].start()
     scale = scales[0, :, 0:1]
 
     rs_copies = []
@@ -628,11 +628,36 @@
 
     some = dvr.at[pl.ds(1, nl - 1)]
     remote(some, some, dv_send, dv_recv, leaf=me_l).wait_recv()
-    outs.append(pltpu.make_async_copy(dvr, dv_out, out_sem.at[2]))
-    outs[2].start()
+    shape = (nodes * rows, 128)
+    at_node = lax.broadcasted_iota(jnp.int32, shape, 0) // rows
+    same_row = lax.broadcasted_iota(jnp.int32, shape, 0) % rows == (
+        lax.broadcasted_iota(jnp.int32, shape, 1) % rows
+    )
+    scaled = cw[...].reshape(nl, 128)
+    picked = hot[...].reshape(nl, 128).astype(BF16)
+    high = scaled.astype(BF16)
+    rest = (scaled - high.astype(F32)).astype(BF16)
+    sums = (dot_tn(picked, high) + dot_tn(picked, rest))[:nodes]
+    spread = jnp.broadcast_to(sums[:, None, :], (nodes, rows, 128)).reshape(shape)
+    spread = jnp.where(same_row, spread, 0.0)
+    high = spread.astype(BF16)
+    rest = (spread - high.astype(F32)).astype(BF16)
+    lines = jnp.concatenate(
+        [jnp.broadcast_to(read[h], (rows, width)) for h in range(GROUP)], 0
+    ).astype(BF16)
+    total_values = dot_nn(high, lines) + dot_nn(rest, lines)
+    for k in range(nl // parts):
+        line = par_slots[k * parts]
+        for b in range(1, parts):
+            line = jnp.where(group == b, par_slots[k * parts + b], line)
+        pick = jnp.where((at_node == line) & same_row, 1.0, 0.0).astype(BF16)
+        total_values += dot_nn(pick, dvr[k * parts : (k + 1) * parts].reshape(128, width))
+    gvs[...] = total_values.astype(BF16).reshape(nodes, rows, width)
+    outs.append(pltpu.make_async_copy(gvs, gv_out, out_sem.at[2]))
+    outs[1].start()
     remote(some, some, dk_send, dk_recv, leaf=me_l).wait_recv()
     outs.append(pltpu.make_async_copy(dkr, dk_out, out_sem.at[3]))
-    outs[3].start()
+    outs[2].start()
 
     for slot in range(2, 6):
         rs_copies[slot].wait_recv()
@@ -640,7 +665,7 @@
     gh[second, :] = (ps[2, second] + rs_r[2].astype(F32) + rs_r[5].astype(F32)).astype(BF16)
 
     outs.append(pltpu.make_async_copy(gh, gh_out, out_sem.at[4]))
-    outs[4].start()
+    outs[3].start()
 
     for copy in ag + ws_copies + gx_copies + rs_copies:
         copy.wait_send()
@@ -659,39 +684,16 @@
         out.wait()
 
 
-def collect_kernel(par, readout, cw, dk_in, dv_in, gh_in, gh, gk, gv, key_total, value_total, sums):
-    nodes, rows, width = gk.shape
-    key_total[...] = jnp.zeros_like(key_total)
-    value_total[...] = jnp.zeros_like(value_total)
-    sums[...] = jnp.zeros_like(sums)
+def collect_kernel(par, dk_in, gv_in, gh_in, gh, gk, gv, total):
+    total[...] = jnp.zeros_like(total)
 
     def add(s, c):
-        node = par[s, 0, 0]
-        key_total[node] += dk_in[s].astype(F32)
-        value_total[node] += dv_in[s].astype(F32)
-        sums[node] += cw[s]
+        total[par[s, 0, 0]] += dk_in[s].astype(F32)
         return c
 
     lax.fori_loop(0, dk_in.shape[0], add, 0, unroll=4)
-    gk[...] = key_total[...].astype(BF16)
-    shape = (1, rows, 128)
-    keep = lax.broadcasted_iota(jnp.int32, shape, 2) % rows == lax.broadcasted_iota(
-        jnp.int32, shape, 1
-    )
-    left = jnp.where(keep, sums[...], 0.0).reshape(nodes * rows, 128)
-    high = left.astype(BF16)
-    rest = (left - high.astype(F32)).astype(BF16)
-    right = jnp.concatenate(
-        [
-            jnp.broadcast_to(
-                readout[h * width : (h + 1) * width].astype(F32).reshape(1, width), (rows, width)
-            )
-            for h in range(128 // rows)
-        ],
-        0,
-    ).astype(BF16)
-    extra = dot_nn(high, right) + dot_nn(rest, right)
-    gv[...] = (value_total[...] + extra.reshape(nodes, rows, width)).astype(BF16)
+    gk[...] = total[...].astype(BF16)
+    gv[...] = gv_in[...]
     gh[...] = gh_in[...]
 
 
@@ -772,6 +774,7 @@
         rows_of_all,
         rows_of_all,
         rows_of_all,
+        pltpu.VMEM((nodes, rows, width), BF16),
         pltpu.VMEM((GROUP + 2, 2, tokens, width), BF16),
         pltpu.VMEM((GROUP + 2, 2, tokens, width), BF16),
         pltpu.VMEM((2, 2, tokens, cols), BF16),
@@ -806,17 +809,16 @@
     table = jax.ShapeDtypeStruct((nodes, rows, width), BF16)
     per_slot = jax.ShapeDtypeStruct((nl, rows, width), BF16)
     grad_hidden = jax.ShapeDtypeStruct((tokens, feats), BF16)
-    gh, dk, dv, cw, par = pl.pallas_call(
+    gh, dk, gv, par = pl.pallas_call(
         functools.partial(main_kernel, ny),
         out_shape=(
             grad_hidden,
             per_slot,
-            per_slot,
-            jax.ShapeDtypeStruct((nl, 1, 128), F32),
+            table,
             jax.ShapeDtypeStruct((nl, 1, 128), jnp.int32),
         ),
         in_specs=[hbm, hbm, smem, hbm] + [anywhere] * 5 + [hbm] * 3 + [anywhere] * 2,
-        out_specs=(anywhere,) * 5,
+        out_specs=(anywhere,) * 4,
         scratch_shapes=scratch,
         compiler_params=pltpu.CompilerParams(
             collective_id=0, has_side_effects=True, vmem_limit_bytes=58 * 1024 * 1024
@@ -840,15 +842,11 @@
     return pl.pallas_call(
         collect_kernel,
         out_shape=(grad_hidden, table, table),
-        in_specs=[smem] + [vmem] * 5,
+        in_specs=[smem] + [vmem] * 3,
         out_specs=(vmem,) * 3,
-        scratch_shapes=[
-            pltpu.VMEM((nodes, rows, width), F32),
-            pltpu.VMEM((nodes, rows, width), F32),
-            pltpu.VMEM((nodes, 1, 128), F32),
-        ],
+        scratch_shapes=[pltpu.VMEM((nodes, rows, width), F32)],
         compiler_params=pltpu.CompilerParams(vmem_limit_bytes=58 * 1024 * 1024),
-    )(par, readout, cw, dk, dv, gh)
+    )(par, dk, gv, gh)
 
 
 def solution(mesh):

time: 56.3 us -> 55.8 us (level)
  no operation moved by 1% of the time
where the time goes in v5:
time: 55.8 us; the launch traced here: 55.6 us
  Pallas kernels  53.7 us (96%)
  between operations  1.94 us (3%)
    pallas_call x1, Pallas kernels, per_device(): pl.pallas_call(functools.partial(main_kernel, ny), out_shape=(grad_hidden...  51.5 us
    pallas_call x1, Pallas kernels, per_device(): pl.pallas_call(collect_kernel, out_shape=(grad_hidden, table, table), in_...  2.19 us

profile of v5, /device:TPU:32, one launch (start us, length us, event | category | flops | bytes accessed | tf_op | source)
XLA Modules:
  0.0 55.6 jit_solution(6633201655843403180)
XLA Ops:
  1.9 51.5 %shard_map.157 = (bf16[256,512]{1,0:T(8,128)(2,1)}, bf16[32,32,128]{2,1,0:T(8,128)(2,1)}, bf16[32,32,128]{2,1,0:T(8,128)(2,1)}, s32[32,1,128]{2,1,0:T(1,128)}) custom-call(s32[1]{0:T(128)S(6)} %copy.17.parents, s32[1]{0:T(128)S(6)} %copy.18.visits, s32[32]{0:T(128)} %lengths.1, f32[1,128]{1,0:T(1,128)} %constant.2.clone.freq_in, bf16[256,512]{1,0:T(8,128)(2,1)} %hid.1, ...), custom_call_target="tpu_custom_call" | custom-call | tf_op jit(solution)/shard_map/pallas_call | solution.py:812
  53.4 2.2 %shard_map.158 = (bf16[256,512]{1,0:T(8,128)(2,1)}, bf16[32,32,128]{2,1,0:T(8,128)(2,1)}, bf16[32,32,128]{2,1,0:T(8,128)(2,1)}) custom-call(s32[32,1,128]{2,1,0:T(1,128)} %get-tuple-element.7.par, bf16[32,32,128]{2,1,0:T(8,128)(2,1)} %get-tuple-element.8.dk_in, bf16[32,32,128]{2,1,0:T(8,128)(2,1)} %get-tuple-element.9.gv_in, ...), custom_call_target="tpu_custom_call" | custom-call | tf_op jit(solution)/shard_map/pallas_call | solution.py:842
